TPU v7x, 128 devices: a whole 4x4x4 slice. The times are simulated.
128 devices in a mesh: span: 8 (over x, y_lo), stream: 16 (over z, y_hi, core).
Axes of the slice: x: 4, y: 4 (y_hi: 2, y_lo: 2; y = y_hi * 2 + y_lo), z: 4, core: 2. Of those that a mesh axis runs over, the one named last changes fastest.
Arguments:
- adjoint: bfloat16 [3, 48, 512, 2048], P(None, 'stream', 'span'), may hold values from -6 to 6
- saved_grad: bfloat16 [9, 48, 512, 2048], P(None, 'stream', 'span'), may hold values from -4 to 4
- saved_u: bfloat16 [48, 512, 2048], P('stream', 'span'), may hold values from 0.29882812 to 1.6953125
- disk_owner: int32 [48, 512], P('stream', 'span'), may hold values from -1 to 9, as said below
- disk_weight: float32 [48, 512], P('stream', 'span'), may hold values from 0.1 to 1
- row_x: int32 [10], replicated, may hold values from 0 to 2047, as said below
- thrust: float32 [10, 10], replicated, may hold values from 0.5 to 2
- block_inverse: float32 [1024, 12, 4, 4, 256], P(('span', 'stream')), may hold values from -0.6 to 0
Outputs:
- tendency: float32 [3, 2048, 48, 512], P(None, ('span', 'stream'))
Inputs may be any that keep to these rules, and one draw needn't show every extreme that they name: `disk_owner`: each turbine column c covers an elliptical disk of cells, inside the across-wind band of cells y with y * 10 // 512 = c, and at least one cell; -1 elsewhere. `row_x`: Increasing; row r lies in the cells r * (204) to (r + 1) * 204 - 1.
All inputs are finite; a program needn't handle non-finite values.
Results may differ from a plain program's by a relative error of at most 0.0003.
Values sent between devices are 32-bit elements; how exact they have to be, the bound alone decides.
No kernel may reach another device: no remote copies, remote signals or barrier semaphores. Data moves between devices by JAX's collectives and lax.ppermute only.
A program may use at most 128 MiB of HBM per device.

v0:
```python
import math

import jax
import jax.numpy as jnp
from jax import lax
from jax.sharding import PartitionSpec as P

NX = 2048
NY = 512
COLS = 10


def derive_x(operand, wavenumber):
    scale = wavenumber[:, None, None, None]
    cosine = operand[..., :, 0, :, :, :]
    sine = operand[..., :, 1, :, :, :]
    return jnp.stack([scale * sine, -scale * cosine], axis=-4)


def derive_y(operand, wavenumber):
    cosine = operand[..., 0, :]
    sine = operand[..., 1, :]
    return jnp.stack([wavenumber * sine, -wavenumber * cosine], axis=-2)


def derive_z(operand):
    padded = jnp.pad(operand, ((0, 0), (0, 0), (1, 1), (0, 0), (0, 0)))
    return 0.5 * (padded[:, :, 2:] - padded[:, :, :-2])


def solve_levels(right_side, inverses):
    modes, _, levels, _, halves = right_side.shape
    blocks = levels // 4
    grouped = right_side.reshape(modes, 2, blocks, 4, 2, halves).transpose(2, 3, 0, 1, 4, 5)
    matrices = inverses.transpose(1, 2, 3, 0, 4)[:, :, :, :, None, None, :]

    def forward(running, pieces):
        segment, inverse_block = pieces
        first = segment[0] - running
        segment = jnp.concatenate([first[None], segment[1:]], axis=0)
        solved = jnp.sum(inverse_block * segment[None], axis=1)
        return (solved[3], solved)

    start = jnp.zeros((modes, 2, 2, halves), jnp.float32)
    _, partial_out = lax.scan(forward, start, (grouped, matrices))

    def backward(running, pieces):
        solved, inverse_block = pieces
        result = solved - inverse_block[:, 3] * running[None]
        return (result[0], result)

    _, levels_out = lax.scan(backward, start, (partial_out, matrices), reverse=True)
    return levels_out.transpose(2, 3, 0, 1, 4, 5).reshape(modes, 2, levels, 2, halves)


def project(spectrum, inverses, along_wind, across_wind):
    modes = along_wind.shape[0]
    halves = across_wind.shape[0]
    levels = spectrum.shape[2]
    parts = spectrum.reshape(3, modes, 2, levels, 2, halves)
    divergence = (
        derive_x(parts[0], along_wind) + derive_y(parts[1], across_wind) + derive_z(parts[2])
    )
    pressure = solve_levels(divergence, inverses)
    gradient = jnp.stack(
        [derive_x(pressure, along_wind), derive_y(pressure, across_wind), derive_z(pressure)]
    )
    return (parts - gradient).reshape(spectrum.shape)


def wave_table(length):
    positions = jnp.arange(length, dtype=jnp.int32)
    basis = jnp.arange(length, dtype=jnp.int32)
    phase = positions[:, None] * (basis // 2)[None, :] % length
    angle = phase.astype(jnp.float32) * (2.0 * math.pi / length)
    values = jnp.where((basis % 2)[None, :] == 0, jnp.cos(angle), jnp.sin(angle))
    return values / math.sqrt(length)


def cross_table(length):
    half_count = length // 2
    positions = jnp.arange(length, dtype=jnp.int32)
    basis = jnp.arange(length, dtype=jnp.int32)
    phase = positions[:, None] * (basis % half_count)[None, :] % length
    angle = phase.astype(jnp.float32) * (2.0 * math.pi / length)
    values = jnp.where((basis // half_count)[None, :] == 0, jnp.cos(angle), jnp.sin(angle))
    return values / math.sqrt(length)


def body(adjoint, saved_grad, saved_u, disk_owner, disk_weight, row_x, thrust, block_inverse):
    exact_mode = lax.Precision.HIGHEST
    adjoint_wide = adjoint.astype(jnp.float32)
    coupling = jnp.stack(
        [
            sum(
                (
                    adjoint_wide[partner] * saved_grad[3 * component + partner].astype(jnp.float32)
                    for partner in range(3)
                )
            )
            for component in range(3)
        ]
    )
    columns = jnp.arange(COLS, dtype=jnp.int32)
    weighted = jnp.where(
        disk_owner[:, :, None] == columns[None, None, :], disk_weight[:, :, None], 0.0
    )
    column_speed = jnp.take(saved_u, row_x, axis=2).astype(jnp.float32)
    column_adjoint = jnp.take(adjoint[0], row_x, axis=2).astype(jnp.float32)
    speed_part = jnp.einsum("zyr,zyc->rc", column_speed, weighted, precision=exact_mode)
    adjoint_part = jnp.einsum("zyr,zyc->rc", column_adjoint, weighted, precision=exact_mode)
    area_part = jnp.sum(weighted, axis=(0, 1))
    speed_sum, adjoint_sum, disk_area = lax.psum(
        (speed_part, adjoint_part, area_part), ("span", "stream")
    )
    disk_speed = speed_sum / disk_area
    disk_adjoint = adjoint_sum / disk_area
    disk_coeff = -thrust * disk_speed * (1.5 * disk_speed + disk_adjoint)
    cell_term = jnp.einsum("zyc,rc->zyr", weighted, disk_coeff, precision=exact_mode)
    along_table = wave_table(NX)
    placement = (jnp.arange(NX, dtype=jnp.int32)[None, :] == row_x[:, None]).astype(jnp.float32)
    extra = jnp.einsum("zyr,rx->zyx", cell_term, placement, precision=exact_mode)
    source = jnp.concatenate([(coupling[0] + extra)[None], coupling[1:]], axis=0)
    spectrum = jnp.einsum("czyx,xb->cbzy", source, along_table, precision=exact_mode)
    across_table = cross_table(NY)
    gathered = lax.all_to_all(spectrum, "span", split_axis=1, concat_axis=3, tiled=True)
    gathered = jnp.einsum("cbzy,yq->cbzq", gathered, across_table, precision=exact_mode)
    spectrum = lax.all_to_all(gathered, "stream", split_axis=1, concat_axis=2, tiled=True)
    modes = spectrum.shape[1] // 2
    first_mode = lax.axis_index(("span", "stream")) * modes
    mode_index = (first_mode + jnp.arange(modes, dtype=jnp.int32)).astype(jnp.float32)
    along_wind = 2.0 * math.pi * mode_index / NX
    across_wind = 2.0 * math.pi * jnp.arange(NY // 2, dtype=jnp.float32) / NY
    return project(spectrum, block_inverse, along_wind, across_wind)


def solution(mesh):
    in_specs = (
        P(None, "stream", "span", None),
        P(None, "stream", "span", None),
        P("stream", "span", None),
        P("stream", "span"),
        P("stream", "span"),
        P(),
        P(),
        P(("span", "stream"), None, None, None, None),
    )
    out_specs = P(None, ("span", "stream"), None, None)
    return jax.shard_map(body, mesh=mesh, in_specs=in_specs, out_specs=out_specs, check_vma=False)
```

profile of v0, /device:TPU:1, one launch (start us, length us, event | category | flops | bytes accessed | tf_op | source)
XLA Modules:
  0.0 530.0 jit_solution(11849517466777011555)
XLA Ops:
  1.3 4.5 convert_element_type.62
  5.9 2.5 copy.84
  8.4 1.4 copy.56
  9.8 2.2 gather_fusion.1
  13.1 4.8 multiply_add_fusion.1
  17.8 69.0 %all-reduce.2 = (f32[10,10]{1,0:T(8,128)S(1)}, f32[10,10]{1,0:T(8,128)S(1)}, f32[10]{0:T(128)S(1)}) all-reduce(f32[10,10]{1,0:T(8,128)S(1)} %convolution_bitcast_fusion, f32[10,10]{1,0:T(8,128)S(1)} %convolution_bitcast_fusion.1, f32[10]{0:T(128)S(1)} %select_reduce_fusion), channel_id=1, replica_groups=mesh['span'=8,'stream'=16] {'span','stream'}, use_global_device_ids=true, to_apply=%region_3.5 | all-reduce | flops 210 | bytes 1680 | tf_op jit(solution)/shard_map/psum | solution.py:113
  87.0 4.2 fusion.34
  91.6 98.4 %fusion.29 = f32[3,2048,3,64]{1,3,2,0:T(8,128)} fusion(s32[2048]{0:T(1024)S(1)} %add_select_fusion.2, pred[2048]{0:T(1024)(128)(4,1)S(1)} %fusion.76, f32[3,3,64,2048]{3,2,1,0:T(8,128)S(1)} %fusion.126), kind=kOutput, calls=%fused_computation.47 | convolution fusion | flops 29058138112 | bytes 9447424 | tf_op jit(solution)/shard_map/czyx,xb->cbzy/dot_general | solution.py:124
  190.0 11.7 %copy.60 = f32[3,2048,3,64]{3,2,0,1:T(4,128)} copy(f32[3,2048,3,64]{1,3,2,0:T(8,128)} %fusion.29) | data formatting | bytes 9437184 | tf_op jit(solution)/shard_map/czyx,xb->cbzy/transpose | solution.py:124
  201.7 13.1 %reshape.147 = f32[8,1,147456]{2,1,0:T(1,128)} reshape(f32[2048,3,3,64]{3,2,1,0:T(4,128)} %bitcast.124) | data formatting | bytes 9437184
  214.8 4.6 all-to-all-start
  219.5 65.9 %all-to-all-done = f32[8,1,147456]{2,1,0:T(1,128)} async-done(((f32[8,1,147456]{2,1,0:T(1,128)}), f32[8,1,147456]{2,1,0:T(1,128)}, u32[]{:S(2)}, u32[]{:S(2)}) %all-to-all-start) | async-done | bytes 4718624 | tf_op jit(solution)/shard_map/all_to_all | solution.py:126
  285.9 15.7 %reduce = f32[8,147456]{1,0:T(8,128)} reduce(f32[8,1,147456]{2,1,0:T(1,128)} %all-to-all-done, f32[]{:T(128)} %broadcast.273), dimensions={1}, to_apply=%all_to_all.24.reduce_sub_computation | reduce | bytes 9437188 | tf_op jit(solution)/shard_map/all_to_all | solution.py:126
  301.5 13.7 %reshape.148 = f32[2048,3,3,64]{3,2,1,0:T(4,128)} reshape(f32[8,147456]{1,0:T(8,128)} %reduce) | data formatting | bytes 9437184
  315.2 11.6 %copy.81 = f32[3,8,256,3,64]{2,4,1,3,0:T(8,128)} copy(f32[3,8,256,3,64]{4,3,0,2,1:T(4,128)} %bitcast.125) | data formatting | bytes 9437184 | tf_op jit(solution)/shard_map/all_to_all | solution.py:126
  326.8 14.9 %fusion.39 = f32[3,256,3,512]{3,1,2,0:T(8,128)S(1)} fusion(f32[3,256,3,512]{1,3,2,0:T(8,128)} %bitcast.130, s32[512]{0:T(512)S(1)} %fusion.90, pred[512]{0:T(512)(128)(4,1)S(1)} %fusion.96), kind=kOutput, calls=%fused_computation.67 | convolution fusion | flops 7251951616 | bytes 9439744 | tf_op jit(solution)/shard_map/cbzy,yq->cbzq/dot_general | solution.py:127
  341.7 5.8 %copy.64 = f32[3,256,3,512]{3,2,0,1:T(4,128)} copy(f32[3,256,3,512]{3,1,2,0:T(8,128)S(1)} %fusion.39) | data formatting | bytes 9437184 | tf_op jit(solution)/shard_map/cbzy,yq->cbzq/dot_general | solution.py:127
  347.5 6.1 %all-to-all-start.1 = ((f32[3,256,3,512]{3,2,0,1:T(4,128)}), f32[3,256,3,512]{3,2,0,1:T(4,128)}, u32[]{:S(2)}, u32[]{:S(2)}) async-start(f32[3,256,3,512]{3,2,0,1:T(4,128)} %copy.64), calls=%async_computation.1 | async-start | bytes 12582912 | tf_op jit(solution)/shard_map/all_to_all | solution.py:128
  353.6 2.3 copy.98
  355.9 71.3 %all-to-all-done.1 = f32[3,256,3,512]{3,2,0,1:T(4,128)} async-done(((f32[3,256,3,512]{3,2,0,1:T(4,128)}), f32[3,256,3,512]{3,2,0,1:T(4,128)}, u32[]{:S(2)}, u32[]{:S(2)}) %all-to-all-start.1) | async-done | bytes 4718624 | tf_op jit(solution)/shard_map/all_to_all | solution.py:128
  427.3 4.3 copy.65
  431.6 2.1 fusion.117
  434.2 1.4 copy.68
  435.6 2.3 squeeze.77
  437.8 2.8 copy.69
  440.6 3.1 squeeze.78
  443.7 1.3 copy.70
  444.9 2.3 squeeze.79
  447.2 1.0 slice_multiply_fusion.7
  448.6 1.7 slice_multiply_fusion.5
  450.3 2.8 fusion.35
  453.4 20.3 %while.28 = (s32[]{:T(128)}, f32[8,2,2,256]{3,0,2,1:T(8,128)S(1)}, f32[12,4,8,2,2,256]{5,2,4,3,1,0:T(8,128)}, f32[12,4,4,8,1,1,256]{6,3,1,2,5,4,0:T(8,128)}, f32...) while((s32[]{:T(128)}, f32[8,2,2,256]{3,0,2,1:T(8,128)S(1)}, ...), condition=%wide.region_6.8_spmd, body=%wide.region_4.7_spmd.sunk | while | flops 270339 | bytes 1541229 | solution.py:45
  453.5 0.9 copy_bitcast_fusion.5
  455.2 0.9 copy_bitcast_fusion.5
  456.9 0.9 copy_bitcast_fusion.5
  458.6 0.9 copy_bitcast_fusion.5
  460.3 0.9 copy_bitcast_fusion.5
  462.0 0.9 copy_bitcast_fusion.5
  463.7 0.9 copy_bitcast_fusion.5
  465.4 0.9 copy_bitcast_fusion.5
  467.1 0.9 copy_bitcast_fusion.5
  468.8 0.9 copy_bitcast_fusion.5
  470.4 0.9 copy_bitcast_fusion.5
  472.1 0.9 copy_bitcast_fusion.5
  474.5 25.1 %while.29 = (s32[]{:T(128)}, f32[8,2,2,256]{3,2,1,0:T(2,128)S(1)}, f32[12,4,8,2,2,256]{5,4,3,2,1,0:T(2,128)S(1)}, f32[12,4,8,2,2,256]{5,2,4,3,1,0:T(8,128)}, f32...) while((s32[]{:T(128)}, f32[8,2,2,256]{3,2,1,0:T(2,128)S(1)}, ...), condition=%wide.region_8.10_spmd, body=%wide.region_7.9_spmd.sunk | while | flops 81923 | bytes 1237093 | solution.py:52
  474.6 1.0 dynamic-slice_bitcast_fusion.6
  475.5 0.9 constant_dynamic-slice_fusion.6
  477.6 0.9 constant_dynamic-slice_fusion.6
  479.7 0.9 constant_dynamic-slice_fusion.6
  481.7 0.9 constant_dynamic-slice_fusion.6
  483.8 0.9 constant_dynamic-slice_fusion.6
  485.8 0.9 constant_dynamic-slice_fusion.6
  487.9 0.9 constant_dynamic-slice_fusion.6
  489.9 0.9 constant_dynamic-slice_fusion.6
  499.7 1.0 slice_multiply_fusion.3
  500.7 2.9 slice_multiply_fusion.1
  503.6 2.0 subtract_multiply_fusion
  505.6 2.7 copy.66
  509.1 1.3 stack.37
  510.4 4.1 pad_maximum_fusion.2
  514.4 3.6 stack.39
  518.1 2.4 stack.40
  520.5 4.4 maximum_subtract_fusion
  524.9 4.9 copy.76
  (195 shorter events, 31.0 us)
Async XLA Ops:
  1.3 4.6 slice-start.2
  5.9 2.6 copy-start.4
  8.4 4.1 copy-start.5
  8.4 4.1 copy-start.6
  13.1 73.8 %copy-start.7 = (f32[10,10]{1,0:T(8,128)S(1)}, f32[10,10]{1,0:T(8,128)}, u32[]{:S(2)}) copy-start(f32[10,10]{1,0:T(8,128)} %param.20) | copy-start | bytes 1204
  13.1 74.0 %copy-start.8 = (s32[10]{0:T(128)S(1)}, s32[10]{0:T(128)}, u32[]{:S(2)}) copy-start(s32[10]{0:T(128)} %param.19) | copy-start | bytes 124
  214.8 70.6 %all-to-all-start = ((f32[8,1,147456]{2,1,0:T(1,128)}), f32[8,1,147456]{2,1,0:T(1,128)}, u32[]{:S(2)}, u32[]{:S(2)}) async-start(f32[8,1,147456]{2,1,0:T(1,128)} %reshape.147), calls=%async_computation | async-start | bytes 9437184 | tf_op jit(solution)/shard_map/all_to_all | solution.py:126
  347.5 6.1 %copy-start.3 = (f32[8,12,4,4,256]{4,3,2,1,0:T(4,128)S(1)}, f32[8,12,4,4,256]{4,3,2,1,0:T(4,128)}, u32[]{:S(2)}) copy-start(f32[8,12,4,4,256]{4,3,2,1,0:T(4,128)} %param.21) | copy-start | bytes 4718596
  347.5 79.7 %all-to-all-start.1 = ((f32[3,256,3,512]{3,2,0,1:T(4,128)}), f32[3,256,3,512]{3,2,0,1:T(4,128)}, u32[]{:S(2)}, u32[]{:S(2)}) async-start(f32[3,256,3,512]{3,2,0,1:T(4,128)} %copy.64), calls=%async_computation.1 | async-start | bytes 12582912 | tf_op jit(solution)/shard_map/all_to_all | solution.py:128
  431.6 2.7 copy-start
  447.2 1.4 copy-start.2
  474.5 31.1 %slice-start = ((s8[4718592]{0:T(1024)(128)(4,1)}), s8[524288]{0:T(1024)(128)(4,1)S(1)}, s32[]{:S(2)}) async-start(s8[4718592]{0:T(1024)(128)(4,1)} %bitcast.127), calls=%async_computation.2 | async-start | bytes 1048576
  499.7 5.9 %slice-start.1 = ((s8[4718592]{0:T(1024)(128)(4,1)}), s8[4194304]{0:T(1024)(128)(4,1)S(1)}, s32[]{:S(2)}) async-start(s8[4718592]{0:T(1024)(128)(4,1)} %bitcast.127), calls=%async_computation.3 | async-start | bytes 8388608
  514.4 3.6 copy-start.1
where the time goes:
time: 536 us; the launch traced here: 530 us
  local copies, waits for them, and re-layouts  143 us (27%)
  waiting for transfers between devices  137 us (26%)
  matrix products  118 us (22%)
  blocking collectives  69 us (13%)
  other arithmetic  50 us (9%)
  starting transfers between devices  10.7 us (2%)
    dot_general x1, matrix products, body(): jnp.einsum('czyx,xb->cbzy', source, along_table, precision=exact_mode)  98.4 us
    all_to_all x1, waiting for transfers between devices, body(): lax.all_to_all(gathered, 'stream', split_axis=1, concat_axis=2, tiled=True)  71.3 us
    psum x1, blocking collectives, body(): lax.psum((speed_part, adjoint_part, area_part), ('span', 'stream'))  69 us
    all_to_all x1, waiting for transfers between devices, body(): lax.all_to_all(spectrum, 'span', split_axis=1, concat_axis=3, tiled=True)  65.9 us
    unnamed x27, local copies, waits for them, and re-layouts  33.9 us
    all_to_all x1, other arithmetic, body(): lax.all_to_all(spectrum, 'span', split_axis=1, concat_axis=3, tiled=True)  15.7 us
    dot_general x1, matrix products, body(): jnp.einsum('cbzy,yq->cbzq', gathered, across_table, precision=exact_mode)  14.9 us
    all_to_all x2, local copies, waits for them, and re-layouts, body(): lax.all_to_all(spectrum, 'span', split_axis=1, concat_axis=3, tiled=True)  12 us
  transfers between devices with their start and end apart: 2, of which 2 were waited for; matrix products, arithmetic and copies ran while one was open for 0% of the time, Pallas kernels for 0%

commit v1 on v0

v1 whole, which is shorter than its diff:
```python
import functools
import math

import jax
import jax.numpy as jnp
import ml_dtypes
import numpy as np
from jax import lax
from jax.experimental import pallas as pl
from jax.experimental.pallas import tpu as pltpu
from jax.sharding import PartitionSpec as P

NX = 2048
NY = 512
NZ = 48
ROWS = 10
COLS = 10
HALF = NX // 2
BLOCKS = NZ // 4
WIDE = 1280
CHUNK = 256
F32 = jnp.float32
BF16 = jnp.bfloat16
VMEM_BYTES = 56 * 1024 * 1024


def split_table(values):
    high = values.astype(ml_dtypes.bfloat16)
    low = (values - high.astype(np.float64)).astype(ml_dtypes.bfloat16)
    return high, low


@functools.lru_cache(maxsize=None)
def along_tables():
    row = np.arange(HALF)
    out = []
    for parity in range(2):
        mode = 8 * (row // 8) + 2 * (row % 4) + parity
        sine = (row // 4) % 2
        phase = mode[:, None] * np.arange(HALF)[None, :] % NX
        angle = phase * (2.0 * np.pi / NX)
        out.append(np.where(sine[:, None] == 0, np.cos(angle), np.sin(angle)) / np.sqrt(NX))
    return split_table(np.stack(out))


@functools.lru_cache(maxsize=None)
def across_tables():
    basis = np.arange(NY)
    phase = np.arange(NY)[:, None] * (basis % (NY // 2))[None, :] % NY
    angle = phase * (2.0 * np.pi / NY)
    values = np.where((basis // (NY // 2))[None, :] == 0, np.cos(angle), np.sin(angle))
    return split_table(values / np.sqrt(NY))


def split(value):
    high = value.astype(BF16)
    return high, (value - high.astype(F32)).astype(BF16)


def dot_nt(left, right):
    return lax.dot_general(left, right, (((1,), (1,)), ((), ())), preferred_element_type=F32)


def dot_nn(left, right):
    return jnp.dot(left, right, preferred_element_type=F32)


def along_kernel(
    row_x, first_column, adjoint, grad, saved_u, owner, weight, table_high, table_low,
    out, source_high, source_low, tail_high, tail_low, onehot, extra,
):
    step = pl.program_id(0)

    @pl.when(step == 0)
    def _():
        lane = lax.broadcasted_iota(jnp.int32, (1, 128), 1)
        wanted = jnp.full((1, 128), -1, jnp.int32)
        for r in range(ROWS):
            wanted = jnp.where(lane == r, row_x[r], wanted)
        cell = lax.broadcasted_iota(jnp.int32, (NX, 128), 0)
        onehot[...] = jnp.where(cell == wanted, 1.0, 0.0).astype(BF16)
        extra[...] = jnp.zeros((8, 128), F32)
        tail_high[...] = jnp.zeros(tail_high.shape, BF16)
        tail_low[...] = jnp.zeros(tail_low.shape, BF16)

    for level in range(3):

        @pl.when(step == level)
        def _(level=level):
            velocity = [adjoint[j, 0].astype(F32) for j in range(3)]
            for i in range(3):
                value = velocity[0] * grad[3 * i, 0].astype(F32)
                for j in range(1, 3):
                    value = value + velocity[j] * grad[3 * i + j, 0].astype(F32)
                left, right = value[:, :HALF], value[:, HALF:]
                pair = 3 * i + level
                for parity, folded in enumerate((left + right, left - right)):
                    high, low = split(folded)
                    if pair < 8:
                        source_high[parity, pl.ds(64 * pair, 64)] = high
                        source_low[parity, pl.ds(64 * pair, 64)] = low
                    else:
                        tail_high[parity, pl.ds(64 * parity, 64)] = high
                        tail_low[parity, pl.ds(64 * parity, 64)] = low
            column_u = dot_nn(saved_u[0], onehot[...])
            column_a = dot_nn(adjoint[0, 0], onehot[...])
            lane = lax.broadcasted_iota(jnp.int32, (64, 128), 1)
            column_u = jnp.where(lane == ROWS, 1.0, column_u).astype(BF16)
            column_a = column_a.astype(BF16)
            own = owner[level : level + 1, :]
            heavy = weight[level : level + 1, :]
            masked = jnp.where(own >= 0, heavy, 0.0)
            row = lax.broadcasted_iota(jnp.int32, (8, 64), 0)
            rest = jnp.where(own == first_column[0] + row % 2, heavy, 0.0)
            sum_u = jnp.zeros((8, 128), F32)
            sum_a = jnp.zeros((8, 128), F32)
            for _ in range(3):
                part = rest.astype(BF16)
                rest = rest - part.astype(F32)
                sum_u = sum_u + dot_nn(part, column_u)
                sum_a = sum_a + dot_nn(part, column_a)
            row = lax.broadcasted_iota(jnp.int32, (8, 128), 0)
            added = jnp.where(row < 2, sum_u, jnp.where(row < 4, sum_a, 0.0))
            padded = jnp.concatenate([masked, jnp.zeros((1, 64), F32)], axis=1)
            extra[...] += jnp.where(row == 4 + level, padded, added)

    @pl.when(step >= 3)
    def _():
        dests = CHUNK // 8
        tail = jnp.zeros((CHUNK, 128), F32)
        for parity in range(2):
            high, low = table_high[parity], table_low[parity]
            body = dot_nt(high, source_high[parity])
            body = body + dot_nt(high, source_low[parity])
            body = body + dot_nt(low, source_high[parity])
            out[:, :, 512 * parity : 512 * parity + 512] = body.reshape(dests, 8, 512)
            tail = tail + dot_nt(high, tail_high[parity])
            tail = tail + dot_nt(high, tail_low[parity])
            tail = tail + dot_nt(low, tail_high[parity])
        out[:, :, 1024:1152] = tail.reshape(dests, 8, 128)
        out[:, :, 1152:1280] = jnp.broadcast_to(extra[...][None], (dests, 8, 128))


def along(adjoint, grad, saved_u, owner, weight, row_x, first_column):
    table_high, table_low = along_tables()
    chunks = HALF // CHUNK

    def level_of(step):
        return jnp.minimum(step, 2)

    def chunk_of(step):
        return jnp.maximum(step - 3, 0)

    return pl.pallas_call(
        along_kernel,
        grid=(3 + chunks,),
        out_shape=jax.ShapeDtypeStruct((128, 8, WIDE), F32),
        in_specs=[
            pl.BlockSpec(memory_space=pltpu.SMEM),
            pl.BlockSpec(memory_space=pltpu.SMEM),
            pl.BlockSpec((3, 1, 64, NX), lambda s: (0, level_of(s), 0, 0)),
            pl.BlockSpec((9, 1, 64, NX), lambda s: (0, level_of(s), 0, 0)),
            pl.BlockSpec((1, 64, NX), lambda s: (level_of(s), 0, 0)),
            pl.BlockSpec((3, 64), lambda s: (0, 0)),
            pl.BlockSpec((3, 64), lambda s: (0, 0)),
            pl.BlockSpec((2, CHUNK, HALF), lambda s: (0, chunk_of(s), 0)),
            pl.BlockSpec((2, CHUNK, HALF), lambda s: (0, chunk_of(s), 0)),
        ],
        out_specs=pl.BlockSpec((CHUNK // 8, 8, WIDE), lambda s: (chunk_of(s), 0, 0)),
        scratch_shapes=[
            pltpu.VMEM((2, 512, HALF), BF16),
            pltpu.VMEM((2, 512, HALF), BF16),
            pltpu.VMEM((2, 128, HALF), BF16),
            pltpu.VMEM((2, 128, HALF), BF16),
            pltpu.VMEM((NX, 128), BF16),
            pltpu.VMEM((8, 128), F32),
        ],
        compiler_params=pltpu.CompilerParams(vmem_limit_bytes=VMEM_BYTES),
        name="along",
    )(row_x, first_column, adjoint, grad, saved_u, owner, weight,
      jnp.asarray(table_high), jnp.asarray(table_low))


def signed_x(value, scale):
    return jnp.concatenate(
        [scale[c] * pltpu.roll(value[8 * c : 8 * c + 8], 4, 0) for c in range(2)], axis=0
    )


def signed_y(value, scale):
    return jnp.concatenate([scale * value[:, 256:], -scale * value[:, :256]], axis=1)


def across_kernel(
    received, extras, thrust, row_basis, wave_x, wave_y, inverses, table_high, table_low,
    out, spectrum, solved, grid_high, grid_low, forced, heavy, above,
):
    step = pl.program_id(0)
    low_half = lax.broadcasted_iota(jnp.int32, (1, 1, 128), 2) < 64

    @pl.when(step == 0)
    def _():
        all_extras = extras[...].reshape(8, 16, 8, 128)
        total = jnp.sum(all_extras, axis=1)
        column = lax.broadcasted_iota(jnp.int32, (16, 128), 0)
        sum_u = jnp.zeros((16, 128), F32)
        sum_a = jnp.zeros((16, 128), F32)
        for s in range(8):
            for other in range(2):
                hit = column == 5 * s // 4 + other
                sum_u = sum_u + jnp.where(hit, total[s, other : other + 1, :], 0.0)
                sum_a = sum_a + jnp.where(hit, total[s, 2 + other : 3 + other, :], 0.0)
        lane = lax.broadcasted_iota(jnp.int32, (16, 128), 1)
        valid = (lane < ROWS) & (column < COLS)
        area = jnp.where(valid, sum_u[:, ROWS : ROWS + 1], 1.0)
        speed = sum_u / area
        reverse = sum_a / area
        coeff = jnp.where(valid, -thrust[...] * speed * (1.5 * speed + reverse), 0.0)
        cell = lax.broadcasted_iota(jnp.int32, (16, NY), 1)
        band = lax.broadcasted_iota(jnp.int32, (16, NY), 0)
        spread = jnp.where(cell * COLS // NY == band, 1.0, 0.0).astype(F32)
        exact = lax.Precision.HIGHEST
        per_column = lax.dot_general(
            row_basis[...], coeff, (((1,), (1,)), ((), ())), precision=exact,
            preferred_element_type=F32,
        )
        forced[...] = jnp.dot(per_column, spread, precision=exact, preferred_element_type=F32)
        for j in range(4):
            left = all_extras[2 * j]
            right = pltpu.roll(all_extras[2 * j + 1], 64, 2)
            heavy[:, :, 128 * j : 128 * j + 128] = jnp.where(low_half, left, right)

    @pl.when(step < 4)
    def _():
        for tile in range(9):
            lanes = pl.ds(128 * tile, 128)
            for j in range(4):
                left = received[2 * j, :, :, lanes]
                right = received[2 * j + 1, :, :, lanes]
                values = (
                    jnp.where(low_half, left, pltpu.roll(right, 64, 2)),
                    jnp.where(low_half, pltpu.roll(left, 64, 2), right),
                )
                for side in range(2):
                    if tile < 8:
                        parity, pair = tile // 4, 2 * (tile % 4) + side
                    else:
                        parity, pair = side, 8
                    component, inner = pair // 3, pair % 3
                    value = values[side]
                    cells = slice(128 * j, 128 * j + 128)
                    if component == 0:
                        disk = heavy[pl.ds(4 * step, 4), 4 + inner : 5 + inner, cells]
                        value = value + disk * forced[8 * parity : 8 * parity + 8, cells][None]
                    for t in range(4):
                        spectrum[component, 12 * step + 3 * t + inner, 8 * parity : 8 * parity + 8, cells] = value[t]
        for component in range(3):
            high, low = split(spectrum[component, pl.ds(12 * step, 12)].reshape(192, NY))
            grid_high[pl.ds(192 * component, 192)] = high
            grid_low[pl.ds(192 * component, 192)] = low
        result = dot_nn(grid_high[...], table_high[...])
        result = result + dot_nn(grid_low[...], table_high[...])
        result = result + dot_nn(grid_high[...], table_low[...])
        spectrum[:, pl.ds(12 * step, 12)] = result.reshape(3, 12, 16, NY)

    scale_x = [wave_x[c] for c in range(2)]
    scale_y = wave_y[0:1, :]

    def forward(block, carry):
        entries = []
        for i in range(4):
            z = 4 * block + i
            up = spectrum[2, jnp.minimum(z + 1, NZ - 1)]
            up = jnp.where(z + 1 < NZ, up, 0.0)
            down = spectrum[2, jnp.maximum(z - 1, 0)]
            down = jnp.where(z > 0, down, 0.0)
            entries.append(
                signed_x(spectrum[0, z], scale_x)
                + signed_y(spectrum[1, z], scale_y)
                + 0.5 * (up - down)
            )
        entries[0] = entries[0] - carry
        last = None
        for i in range(4):
            halves = []
            for q in range(2):
                total = inverses[block, 4 * i] * entries[0][:, 256 * q : 256 * q + 256]
                for j in range(1, 4):
                    total = total + inverses[block, 4 * i + j] * entries[j][:, 256 * q : 256 * q + 256]
                halves.append(total)
            last = jnp.concatenate(halves, axis=1)
            solved[4 * block + i] = last
        return last

    @pl.when(step == 3)
    def _():
        lax.fori_loop(0, BLOCKS, forward, jnp.zeros((16, NY), F32))
        above[...] = jnp.zeros((16, NY), F32)

    def corrected(block, i, running):
        column = inverses[block, 4 * i + 3]
        return solved[4 * block + i] - jnp.concatenate([column, column], axis=1) * running

    @pl.when(step >= 4)
    def _():
        group = 9 - step
        first = 2 * group
        upper = above[...]
        running = upper
        pressure = [None] * 8
        for half in (1, 0):
            for i in range(4):
                pressure[4 * half + i] = corrected(first + half, i, running)
            running = pressure[4 * half]
        before = corrected(jnp.maximum(first - 1, 0), 3, running)
        before = jnp.where(group > 0, before, 0.0)
        above[...] = running
        pressure = [before] + pressure + [upper]
        for component in range(3):
            rows = []
            for z in range(8):
                here = pressure[z + 1]
                if component == 0:
                    slope = signed_x(here, scale_x)
                elif component == 1:
                    slope = signed_y(here, scale_y)
                else:
                    slope = 0.5 * (pressure[z + 2] - pressure[z])
                rows.append(spectrum[component, 8 * group + z] - slope)
            for m in range(16):
                source = 8 * ((m // 2) % 2) + 4 * (m % 2) + m // 4
                out[component, m] = jnp.concatenate(
                    [rows[z][source : source + 1] for z in range(8)], axis=0
                )


def across(received, thrust, row_basis, wave_x, wave_y, inverses):
    table_high, table_low = across_tables()

    def whole(shape):
        return pl.BlockSpec(shape, lambda s: (0,) * len(shape))

    return pl.pallas_call(
        across_kernel,
        grid=(10,),
        out_shape=jax.ShapeDtypeStruct((3, 16, NZ, NY), F32),
        in_specs=[
            pl.BlockSpec((8, 4, 8, WIDE), lambda s: (0, jnp.minimum(s, 3), 0, 0)),
            pl.BlockSpec((8, 16, 8, 128), lambda s: (0, 0, 0, 9)),
            whole((16, 128)),
            whole((16, 128)),
            whole((2, 8, 1)),
            whole((1, 256)),
            whole((BLOCKS, 16, 16, 256)),
            whole((NY, NY)),
            whole((NY, NY)),
        ],
        out_specs=pl.BlockSpec((3, 16, 8, NY), lambda s: (0, 0, jnp.minimum(9 - s, 5), 0)),
        scratch_shapes=[
            pltpu.VMEM((3, NZ, 16, NY), F32),
            pltpu.VMEM((NZ, 16, NY), F32),
            pltpu.VMEM((576, NY), BF16),
            pltpu.VMEM((576, NY), BF16),
            pltpu.VMEM((16, NY), F32),
            pltpu.VMEM((16, 8, NY), F32),
            pltpu.VMEM((16, NY), F32),
        ],
        compiler_params=pltpu.CompilerParams(vmem_limit_bytes=VMEM_BYTES),
        name="across",
    )(received, received, thrust, row_basis, wave_x, wave_y, inverses,
      jnp.asarray(table_high), jnp.asarray(table_low))


def body(adjoint, saved_grad, saved_u, disk_owner, disk_weight, row_x, thrust, block_inverse):
    axes = ("span", "stream")
    span = lax.axis_index("span")
    first_column = (5 * span // 4).astype(jnp.int32).reshape(1)
    sent = along(adjoint, saved_grad, saved_u, disk_owner, disk_weight, row_x, first_column)
    received = lax.all_to_all(sent, axes, split_axis=0, concat_axis=0, tiled=True)

    first_mode = lax.axis_index(axes) * 8
    row = jnp.arange(16, dtype=jnp.int32)
    mode = first_mode + 2 * (row % 4) + row // 8
    sine = (row // 4) % 2
    wave = 2.0 * math.pi * mode.astype(F32) / NX
    wave_x = jnp.where(sine == 0, wave, -wave).reshape(2, 8, 1)
    wave_y = (2.0 * math.pi * jnp.arange(NY // 2, dtype=F32) / NY).reshape(1, 256)
    angle = (mode[:, None] * row_x[None, :] % NX).astype(F32) * (2.0 * math.pi / NX)
    basis = jnp.where(sine[:, None] == 0, jnp.cos(angle), jnp.sin(angle)) / math.sqrt(NX)
    row_basis = jnp.pad(basis, ((0, 0), (0, 128 - ROWS)))
    thrust_t = jnp.pad(thrust.T, ((0, 16 - COLS), (0, 128 - ROWS)))
    folded = block_inverse.reshape(4, 2, BLOCKS, 16, 256).transpose(2, 3, 1, 0, 4)
    inverses = jnp.broadcast_to(
        folded[:, :, :, None], (BLOCKS, 16, 2, 2, 4, 256)
    ).reshape(BLOCKS, 16, 16, 256)
    return across(
        received.reshape(8, 16, 8, WIDE), thrust_t, row_basis, wave_x, wave_y, inverses
    )


def solution(mesh):
    in_specs = (
        P(None, "stream", "span", None),
        P(None, "stream", "span", None),
        P("stream", "span", None),
        P("stream", "span"),
        P("stream", "span"),
        P(),
        P(),
        P(("span", "stream"), None, None, None, None),
    )
    out_specs = P(None, ("span", "stream"), None, None)
    return jax.shard_map(body, mesh=mesh, in_specs=in_specs, out_specs=out_specs, check_vma=False)
```

time: 536 us -> 113 us (0.21); the launches traced: 530 us -> 112 us
  local copies, waits for them, and re-layouts: 143 us -> 6.17 us
  matrix products: 118 us -> 0 us
  waiting for transfers between devices: 137 us -> 58.7 us
  blocking collectives: 69 us -> 0 us
  other arithmetic: 50 us -> 1.29 us
  Pallas kernels: 0 us -> 34.3 us
    dot_general x6 -> x0, matrix products: 118 us -> none  [the longest x1 98.4 us: body(): jnp.einsum('czyx,xb->cbzy', source, along_table, precision=exact_mode)]
    all_to_all x2 -> x1, waiting for transfers between devices: 137 us -> 58.7 us  [body(): lax.all_to_all(sent, axes, split_axis=0, concat_axis=0, tiled=True)]
    psum x1 -> x0, blocking collectives: 69 us -> none  [body(): lax.psum((speed_part, adjoint_part, area_part), ('span', 'stream'))]
    pallas_call x0 -> x2, Pallas kernels: none -> 34.3 us  [the longest x1 19.9 us: along(): pl.pallas_call(along_kernel, grid=(3 + chunks,), out_shape=jax.ShapeDtype...]
    unnamed x27 -> x7, local copies, waits for them, and re-layouts: 33.9 us -> 0.11 us
    all_to_all x4 -> x0, local copies, waits for them, and re-layouts: 19.1 us -> none  [the longest x2 12 us: body(): lax.all_to_all(spectrum, 'span', split_axis=1, concat_axis=3, tiled=True)]
    squeeze x27 -> x0, local copies, waits for them, and re-layouts: 18.7 us -> none  [the longest x12 11.1 us: solve_levels(): _, partial_out = lax.scan(forward, start, (grouped, matrices))]
    all_to_all x1 -> x0, other arithmetic: 15.7 us -> none  [body(): lax.all_to_all(spectrum, 'span', split_axis=1, concat_axis=3, tiled=True)]
  transfers between devices with their start and end apart: 2 -> 1, of which waited for: 2 -> 1; matrix products, arithmetic and copies ran while one was open for 0% -> 7% of each run, Pallas kernels for 0% -> 0%
where the time goes in v1:
time: 113 us; the launch traced here: 112 us
  waiting for transfers between devices  58.7 us (52%)
  Pallas kernels  34.3 us (30%)
  starting transfers between devices  11.9 us (11%)
  local copies, waits for them, and re-layouts  6.17 us (5%)
  other arithmetic  1.29 us (1%)
    all_to_all x1, waiting for transfers between devices, body(): lax.all_to_all(sent, axes, split_axis=0, concat_axis=0, tiled=True)  58.7 us
    pallas_call x1, Pallas kernels, along(): pl.pallas_call(along_kernel, grid=(3 + chunks,), out_shape=jax.ShapeDtype...  19.9 us
    pallas_call x1, Pallas kernels, across(): pl.pallas_call(across_kernel, grid=(10,), out_shape=jax.ShapeDtypeStruct(...  14.5 us
    all_to_all x1, starting transfers between devices, body(): lax.all_to_all(sent, axes, split_axis=0, concat_axis=0, tiled=True)  11.9 us
    reshape x1, local copies, waits for them, and re-layouts, body(): inverses = jnp.broadcast_to(folded[:, :, :, None], (BLOCKS, 16, 2, 2, 4,...  2.75 us
  transfers between devices with their start and end apart: 1, of which 1 were waited for; matrix products, arithmetic and copies ran while one was open for 7% of the time, Pallas kernels for 0%

profile of v1, /device:TPU:1, one launch (start us, length us, event | category | flops | bytes accessed | tf_op | source)
XLA Modules:
  0.0 112.5 jit_solution(1300583403708255169)
XLA Ops:
  0.0 19.9 %along.1 = f32[128,8,1280]{2,1,0:T(8,128)} custom-call(s32[10]{0:T(128)} %row_x.1, s32[1]{0:T(128)} %bitcast.first_column, bf16[3,3,64,2048]{3,2,1,0:T(8,128)(2,1)} %adjoint.1, bf16[9,3,64,2048]{3,2,1,0:T(8,128)(2,1)} %grad.1, bf16[3,64,2048]{2,1,0:T(8,128)(2,1)} %saved_u.1, s32[3,64]{1,0:T(4,128)} %owner.1, f32[3,64]{1,0:T(4,128)} %weight.1, ...), custom_call_target="tpu_custom_call" | custom-call | tf_op jit(solution)/shard_map/along/pallas_call | solution.py:154
  19.9 0.0 copy-start
  19.9 11.9 %all-to-all-start = ((f32[128,8,1280]{2,1,0:T(8,128)}), f32[128,8,1280]{2,1,0:T(8,128)}, u32[]{:S(2)}, u32[]{:S(2)}) async-start(f32[128,8,1280]{2,1,0:T(8,128)} %along.1), calls=%async_computation | async-start | bytes 10485760 | tf_op jit(solution)/shard_map/all_to_all | solution.py:379
  31.8 0.0 copy-done
  31.8 0.5 reshape.249
  32.4 1.0 copy.14
  33.4 0.5 broadcast_in_dim.11
  34.0 0.0 copy-start.1
  34.0 0.0 copy-start.2
  34.0 2.7 %reshape.250.inverses = f32[12,16,16,256]{3,2,1,0:T(8,128)} reshape(f32[12,16,2,2,4,256]{5,4,3,2,1,0:T(4,128)S(1)} %broadcast_in_dim.11) | data formatting | bytes 6291456 | tf_op jit(solution)/shard_map/reshape | solution.py:395
  36.7 0.0 copy-done.1
  36.7 0.1 copy.13
  36.8 0.0 copy-done.2
  36.8 0.1 select_multiply_fusion
  37.0 0.6 pad.9.row_basis
  37.6 0.6 pad.8.thrust
  38.2 0.5 iota_multiply_fusion.wave_y
  38.7 0.6 negate_select_fusion.wave_x
  39.3 58.7 %all-to-all-done = f32[128,8,1280]{2,1,0:T(8,128)} async-done(((f32[128,8,1280]{2,1,0:T(8,128)}), f32[128,8,1280]{2,1,0:T(8,128)}, u32[]{:S(2)}, u32[]{:S(2)}) %all-to-all-start) | async-done | bytes 5242912 | tf_op jit(solution)/shard_map/all_to_all | solution.py:379
  98.0 14.5 %across.1 = f32[3,16,48,512]{3,2,1,0:T(8,128)} custom-call(f32[8,16,8,1280]{3,2,1,0:T(8,128)} %bitcast.1.received.extras, f32[8,16,8,1280]{3,2,1,0:T(8,128)} %bitcast.1.received.extras, f32[16,128]{1,0:T(8,128)} %pad.8.thrust, f32[16,128]{1,0:T(8,128)} %pad.9.row_basis, f32[2,8,1]{2,1,0:T(8,128)} %negate_select_fusion.wave_x, ...), custom_call_target="tpu_custom_call" | custom-call | tf_op jit(solution)/shard_map/across/pallas_call | solution.py:343
  (2 shorter events, 0.0 us)
Async XLA Ops:
  19.9 11.9 %copy-start = (f32[8,12,4,4,256]{4,3,2,1,0:T(4,128)S(1)}, f32[8,12,4,4,256]{4,3,2,1,0:T(4,128)}, u32[]{:S(2)}) copy-start(f32[8,12,4,4,256]{4,3,2,1,0:T(4,128)} %param.19) | copy-start | bytes 4718596
  19.9 78.1 %all-to-all-start = ((f32[128,8,1280]{2,1,0:T(8,128)}), f32[128,8,1280]{2,1,0:T(8,128)}, u32[]{:S(2)}, u32[]{:S(2)}) async-start(f32[128,8,1280]{2,1,0:T(8,128)} %along.1), calls=%async_computation | async-start | bytes 10485760 | tf_op jit(solution)/shard_map/all_to_all | solution.py:379
  34.0 2.8 %copy-start.1 = (f32[10,10]{1,0:T(8,128)S(1)}, f32[10,10]{1,0:T(8,128)}, u32[]{:S(2)}) copy-start(f32[10,10]{1,0:T(8,128)} %param.18) | copy-start | bytes 1204
  34.0 2.9 %copy-start.2 = (s32[10]{0:T(128)S(1)}, s32[10]{0:T(128)}, u32[]{:S(2)}) copy-start(s32[10]{0:T(128)} %row_x.1) | copy-start | bytes 124

commit v2 on v1

v2 whole, which is shorter than its diff:
```python
import functools
import math

import jax
import jax.numpy as jnp
import ml_dtypes
import numpy as np
from jax import lax
from jax.experimental import pallas as pl
from jax.experimental.pallas import tpu as pltpu
from jax.sharding import PartitionSpec as P

NX = 2048
NY = 512
NZ = 48
ROWS = 10
COLS = 10
HALF = NX // 2
BLOCKS = NZ // 4
DESTS = 128
ROWS_SENT = 74
GROUP = 4 * ROWS_SENT
F32 = jnp.float32
BF16 = jnp.bfloat16
VMEM_BYTES = 58 * 1024 * 1024


def split_table(values):
    high = values.astype(ml_dtypes.bfloat16)
    low = (values - high.astype(np.float64)).astype(ml_dtypes.bfloat16)
    return high, low


def wave_rows(mode, sine, length):
    phase = mode[:, None] * np.arange(length)[None, :] % NX
    angle = phase * (2.0 * np.pi / NX)
    return np.where(sine[:, None] == 0, np.cos(angle), np.sin(angle)) / np.sqrt(NX)


@functools.lru_cache(maxsize=None)
def along_tables():
    row = np.arange(HALF)
    sine, rest = (row // 4) % 2, row % 4
    odd = wave_rows(8 * (row // 8) + 2 * rest + 1, sine, HALF)
    row = np.arange(HALF // 2)
    sine, slot, inner = (row // 4) % 2, (row // 2) % 2, row % 2
    even = [
        wave_rows(8 * (2 * (row // 8) + (slot ^ kind)) + 4 * inner + 2 * kind, sine, HALF // 2)
        for kind in range(2)
    ]
    return np.stack(split_table(odd)), np.stack(split_table(np.stack(even)))


@functools.lru_cache(maxsize=None)
def across_tables():
    basis = np.arange(NY)
    phase = np.arange(NY)[:, None] * (basis % (NY // 2))[None, :] % NY
    angle = phase * (2.0 * np.pi / NY)
    values = np.where((basis // (NY // 2))[None, :] == 0, np.cos(angle), np.sin(angle))
    return np.stack(split_table(values / np.sqrt(NY)))


def split(value):
    high = value.astype(BF16)
    return high, (value - high.astype(F32)).astype(BF16)


def dot_nt(left, right):
    return lax.dot_general(left, right, (((1,), (1,)), ((), ())), preferred_element_type=F32)


def dot_nn(left, right):
    return jnp.dot(left, right, preferred_element_type=F32)


def couple(level, steps, adjoint, grad, highs, lows, tail):
    quarter = NX // 4
    for step in steps:
        rows = pl.ds(pl.multiple_of(16 * step, 16), 16)
        for start in range(0, quarter, 128):
            lanes = [pl.ds(quarter * n + start, 128) for n in range(4)]
            velocity = [[adjoint[j, level, rows, l].astype(F32) for l in lanes] for j in range(3)]
            for i in range(3):
                value = []
                for n, l in enumerate(lanes):
                    total = velocity[0][n] * grad[3 * i, level, rows, l].astype(F32)
                    for j in range(1, 3):
                        total = total + velocity[j][n] * grad[3 * i + j, level, rows, l].astype(F32)
                    value.append(total)
                first, second = value[0] + value[2], value[1] + value[3]
                folded = (value[0] - value[2], value[1] - value[3], first + second, first - second)
                pair = 3 * level + i
                window, place = pair // 4, 64 * (pair % 4)
                for n in range(4):
                    high, low = split(folded[n])
                    target = pl.ds(pl.multiple_of(place + 16 * step, 16), 16)
                    if window < 2:
                        highs[window][target, lanes[n]] = high
                        lows[window][target, lanes[n]] = low
                    else:
                        tail[target, lanes[n]] = high
                        tail[pl.ds(pl.multiple_of(64 + 16 * step, 16), 16), lanes[n]] = low


def along_kernel(
    row_x, first_column, owner, weight, adjoint_hbm, grad_hbm, saved_u_hbm, odd_hbm, even_hbm,
    out, adjoint, grad, saved_u, odd, even, high_0, high_1, low_0, low_1, tail, onehot, outbox, sems,
):
    highs, lows = (high_0, high_1), (low_0, low_1)
    copies = []
    for level in range(3):
        copies.append(pltpu.make_async_copy(adjoint_hbm.at[:, level], adjoint.at[:, level], sems.at[2 * level]))
        copies.append(pltpu.make_async_copy(grad_hbm.at[:, level], grad.at[:, level], sems.at[2 * level + 1]))
    fetch_u = pltpu.make_async_copy(saved_u_hbm, saved_u, sems.at[6])
    fetch_odd = pltpu.make_async_copy(odd_hbm, odd, sems.at[7])
    fetch_even = pltpu.make_async_copy(even_hbm, even, sems.at[8])
    for copy in copies[:4] + [fetch_u] + copies[4:] + [fetch_odd, fetch_even]:
        copy.start()

    lane = lax.broadcasted_iota(jnp.int32, (1, 128), 1) % 16
    wanted = jnp.full((1, 128), -1, jnp.int32)
    for r in range(ROWS):
        wanted = jnp.where(lane == r, row_x[r], wanted)

    def mark(step, _):
        rows = pl.ds(pl.multiple_of(256 * step, 256), 256)
        cell = lax.broadcasted_iota(jnp.int32, (256, 128), 0) + 256 * step
        onehot[rows, :] = jnp.where(cell == wanted, 1.0, 0.0).astype(BF16)
        return 0

    lax.fori_loop(0, NX // 256, mark, 0)

    def couple_rows(level):
        def rows_of(step, _):
            couple(level, (step,), adjoint, grad, highs, lows, tail)
            return 0

        lax.fori_loop(0, 4, rows_of, 0)

    for level in range(3):
        copies[2 * level].wait()
        copies[2 * level + 1].wait()
        if level < 2:
            couple_rows(level)

    fetch_u.wait()
    sum_u = jnp.zeros((8, 128), F32)
    sum_a = jnp.zeros((8, 128), F32)
    masked = []
    for level in range(3):
        column_u = dot_nn(saved_u[level], onehot[...])
        column_a = dot_nn(adjoint[0, level], onehot[...]).astype(BF16)
        column_u = jnp.where(lane == ROWS, 1.0, column_u).astype(BF16)
        own = owner[level : level + 1, :]
        heavy = weight[level : level + 1, :]
        masked.append(jnp.where(own >= 0, heavy, 0.0))
        row = lax.broadcasted_iota(jnp.int32, (8, 64), 0)
        rest = jnp.where(own == first_column[0] + row % 2, heavy, 0.0)
        for _ in range(3):
            part = rest.astype(BF16)
            rest = rest - part.astype(F32)
            sum_u = sum_u + dot_nn(part, column_u)
            sum_a = sum_a + dot_nn(part, column_a)
    place = lax.broadcasted_iota(jnp.int32, (1, 128), 1) // 16
    sums = jnp.where(place == 4, sum_u[0:1], sum_u[1:2])
    sums = jnp.where(place == 6, sum_a[0:1], jnp.where(place == 7, sum_a[1:2], sums))
    last = jnp.concatenate([masked[2], jnp.zeros((1, 64), F32)], axis=1)
    last = jnp.where(place < 4, last, sums)
    extra = jnp.concatenate([jnp.concatenate(masked[:2], axis=1), last], axis=0)

    fetch_odd.wait()
    fetch_even.wait()
    first_slot = lax.broadcasted_iota(jnp.int32, (8, 128), 0) % 4 < 2
    low_half = lax.broadcasted_iota(jnp.int32, (8, 128), 1) < 64
    spans = (pl.ds(0, HALF), pl.ds(HALF, HALF // 2), pl.ds(HALF + HALF // 2, HALF // 2))

    def tables_of(step):
        odd_rows = pl.ds(pl.multiple_of(512 * step, 512), 512)
        even_rows = pl.ds(pl.multiple_of(256 * step, 256), 256)
        return [
            [odd[n, odd_rows, :] for n in range(2)],
            [even[n, 0, even_rows, :] for n in range(2)],
            [even[n, 1, even_rows, :] for n in range(2)],
        ]

    def store(step, dest, tile, value):
        start = ROWS_SENT * (dest % 4) + 8 * tile
        outbox[16 * step + dest // 4, pl.ds(start, 8), :] = value

    def pick(dest, products):
        pair = slice(8 * (dest // 2), 8 * (dest // 2) + 8)
        kinds = (products[1][pair], products[2][pair])
        even_part = jnp.where(first_slot, kinds[dest % 2], kinds[1 - dest % 2])
        return even_part, products[0][8 * dest : 8 * dest + 8]

    def main_part(step, window):
        products = []
        for (high, low), span in zip(tables_of(step), spans):
            body = dot_nt(high, highs[window][:, span])
            body = body + dot_nt(high, lows[window][:, span])
            products.append(body + dot_nt(low, highs[window][:, span]))
        for half in range(2):
            part = [p[:, 128 * half : 128 * half + 128] for p in products]
            for dest in range(64):
                even_part, odd_part = pick(dest, part)
                store(step, dest, 2 * window + half, even_part)
                store(step, dest, 4 + 2 * window + half, odd_part)

    def first(step, _):
        couple(2, (2 * step, 2 * step + 1), adjoint, grad, highs, lows, tail)
        main_part(step, 0)
        return 0

    lax.fori_loop(0, 2, first, 0)

    def send(step):
        part = pl.ds(16 * step, 16)
        return pltpu.make_async_copy(outbox.at[part], out.at[part], sems.at[9 + step])

    def second(step, _):
        products = []
        for (high, low), span in zip(tables_of(step), spans):
            body = dot_nt(high, tail[:, span]) + dot_nt(low, tail[:, span])
            products.append(body + pltpu.roll(body, 64, 1))
        for dest in range(64):
            even_part, odd_part = pick(dest, products)
            store(step, dest, 8, jnp.where(low_half, even_part, odd_part))
            outbox[16 * step + dest // 4, pl.ds(ROWS_SENT * (dest % 4) + 72, 2), :] = extra
        main_part(step, 1)
        send(step).start()
        return 0

    lax.fori_loop(0, 2, second, 0)
    send(0).wait()
    send(1).wait()


def along(adjoint, grad, saved_u, owner, weight, row_x, first_column):
    odd, even = along_tables()
    smem = pl.BlockSpec(memory_space=pltpu.SMEM)
    vmem = pl.BlockSpec(memory_space=pltpu.VMEM)
    hbm = pl.BlockSpec(memory_space=pltpu.HBM)
    return pl.pallas_call(
        along_kernel,
        out_shape=jax.ShapeDtypeStruct((DESTS // 4, GROUP, 128), F32),
        in_specs=[smem, smem, vmem, vmem, hbm, hbm, hbm, hbm, hbm],
        out_specs=hbm,
        scratch_shapes=[
            pltpu.VMEM((3, 3, 64, NX), BF16),
            pltpu.VMEM((9, 3, 64, NX), BF16),
            pltpu.VMEM((3, 64, NX), BF16),
            pltpu.VMEM(odd.shape, BF16),
            pltpu.VMEM(even.shape, BF16),
            pltpu.VMEM((256, NX), BF16),
            pltpu.VMEM((256, NX), BF16),
            pltpu.VMEM((256, NX), BF16),
            pltpu.VMEM((256, NX), BF16),
            pltpu.VMEM((128, NX), BF16),
            pltpu.VMEM((NX, 128), BF16),
            pltpu.VMEM((DESTS // 4, GROUP, 128), F32),
            pltpu.SemaphoreType.DMA((11,)),
        ],
        compiler_params=pltpu.CompilerParams(vmem_limit_bytes=VMEM_BYTES),
        name="along",
    )(row_x, first_column, owner, weight, adjoint, grad, saved_u, jnp.asarray(odd), jnp.asarray(even))


def signed_x(value, scale):
    return jnp.concatenate(
        [scale[c] * pltpu.roll(value[8 * c : 8 * c + 8], 4, 0) for c in range(2)], axis=0
    )


def signed_y(value, scale):
    return jnp.concatenate([scale * value[:, 256:], -scale * value[:, :256]], axis=1)


def across_kernel(
    parity, thrust, row_basis, wave_x, wave_y, received_hbm, inverses_hbm, tables_hbm,
    out, received, inverses, tables, spectrum, solved, grid_high, grid_low, forced, heavy, staged, sems,
):
    fetch = []
    for group in range(4):
        for s in range(8):
            fetch.append(pltpu.make_async_copy(
                received_hbm.at[4 * s + group], received.at[4 * s + group], sems.at[6 + group]
            ))
    fetch_tables = pltpu.make_async_copy(tables_hbm, tables, sems.at[10])
    fetch_inverses = pltpu.make_async_copy(inverses_hbm, inverses, sems.at[11])
    for copy in fetch[:8] + [fetch_tables] + fetch[8:] + [fetch_inverses]:
        copy.start()
    low_half = lax.broadcasted_iota(jnp.int32, (1, 128), 1) < 64
    low_half3 = low_half[None]

    def place(group, t, component):
        for tile in range(9):
            rows = pl.ds(ROWS_SENT * t + 8 * tile, 8)
            for side in range(2):
                kind, pair = (tile // 4, 2 * (tile % 4) + side) if tile < 8 else (side, 8)
                if pair % 3 != component:
                    continue
                inner = pair // 3
                for j in range(4):
                    cells = pl.ds(128 * j, 128)
                    left = received[8 * j + group, rows, :]
                    right = received[8 * j + 4 + group, rows, :]
                    if side == 0:
                        value = jnp.where(low_half, left, pltpu.roll(right, 64, 1))
                    else:
                        value = jnp.where(low_half, pltpu.roll(left, 64, 1), right)
                    if component == 0:
                        disk = heavy[inner, t, group, :, cells]
                        value = value + disk * forced[pl.ds(8 * kind, 8), cells]
                    spectrum[component, 12 * group + 3 * t + inner, pl.ds(8 * kind, 8), cells] = value

    def multiply(parts):
        for n, (component, group) in enumerate(parts):
            high, low = split(spectrum[component, pl.ds(12 * group, 12)].reshape(192, NY))
            grid_high[pl.ds(192 * n, 192)] = high
            grid_low[pl.ds(192 * n, 192)] = low
        result = dot_nn(grid_high[...], tables[0])
        result = result + dot_nn(grid_low[...], tables[0])
        result = result + dot_nn(grid_high[...], tables[1])
        for n, (component, group) in enumerate(parts):
            spectrum[component, pl.ds(12 * group, 12)] = result[192 * n : 192 * n + 192].reshape(12, 16, NY)

    for group in range(4):
        for copy in fetch[8 * group : 8 * group + 8]:
            copy.wait()
        if group == 0:
            fetch_tables.wait()

        for t in range(4):
            place(group, t, 1)
            place(group, t, 2)
        multiply(((1, group), (2, group)))

    total = jnp.zeros((8, 1, 128), F32)
    for t in range(4):
        start = ROWS_SENT * t + 72
        upper = received[:, pl.ds(start, 1), :].reshape(4, 2, 4, 1, 128)
        lower = received[:, pl.ds(start + 1, 1), :]
        total = total + jnp.sum(lower.reshape(8, 4, 1, 128), axis=1)
        lower = lower.reshape(4, 2, 4, 1, 128)
        for j in range(4):
            cells = pl.ds(128 * j, 128)
            left, right = upper[j, 0], upper[j, 1]
            heavy[0, t, :, :, cells] = jnp.where(low_half3, left, pltpu.roll(right, 64, 2))
            heavy[1, t, :, :, cells] = jnp.where(low_half3, pltpu.roll(left, 64, 2), right)
            left, right = lower[j, 0], lower[j, 1]
            heavy[2, t, :, :, cells] = jnp.where(low_half3, left, pltpu.roll(right, 64, 2))
    column = lax.broadcasted_iota(jnp.int32, (16, 128), 0)
    sum_u = jnp.zeros((16, 128), F32)
    sum_a = jnp.zeros((16, 128), F32)
    for s in range(8):
        for other in range(2):
            hit = column == 5 * s // 4 + other
            sum_u = sum_u + jnp.where(hit, pltpu.roll(total[s], 64 - 16 * other, 1), 0.0)
            sum_a = sum_a + jnp.where(hit, pltpu.roll(total[s], 32 - 16 * other, 1), 0.0)
    lane = lax.broadcasted_iota(jnp.int32, (16, 128), 1)
    valid = (lane < ROWS) & (column < COLS)
    area = jnp.where(valid, sum_u[:, ROWS : ROWS + 1], 1.0)
    speed = sum_u / area
    reverse = sum_a / area
    coeff = jnp.where(valid, -thrust[...] * speed * (1.5 * speed + reverse), 0.0)
    cell = lax.broadcasted_iota(jnp.int32, (16, NY), 1)
    band = lax.broadcasted_iota(jnp.int32, (16, NY), 0)
    spread = jnp.where(cell * COLS // NY == band, 1.0, 0.0).astype(F32)
    exact = lax.Precision.HIGHEST
    per_column = lax.dot_general(
        row_basis[...], coeff, (((1,), (1,)), ((), ())), precision=exact, preferred_element_type=F32
    )
    forced[...] = jnp.dot(per_column, spread, precision=exact, preferred_element_type=F32)

    def transform(half, _):
        for group in range(2):
            for t in range(4):
                place(2 * half + group, t, 0)
        multiply(((0, 2 * half), (0, 2 * half + 1)))
        return 0

    lax.fori_loop(0, 2, transform, 0)
    fetch_inverses.wait()

    scale_x = [wave_x[c] for c in range(2)]
    scale_y = wave_y[0:1, :]

    def forward(block, carry):
        entries = []
        for i in range(4):
            z = 4 * block + i
            up = spectrum[2, jnp.minimum(z + 1, NZ - 1)]
            up = jnp.where(z + 1 < NZ, up, 0.0)
            down = spectrum[2, jnp.maximum(z - 1, 0)]
            down = jnp.where(z > 0, down, 0.0)
            entries.append(
                signed_x(spectrum[0, z], scale_x)
                + signed_y(spectrum[1, z], scale_y)
                + 0.5 * (up - down)
            )
        entries[0] = entries[0] - carry
        last = None
        for i in range(4):
            halves = []
            for q in range(2):
                cells = slice(256 * q, 256 * q + 256)
                total = inverses[block, 4 * i] * entries[0][:, cells]
                for j in range(1, 4):
                    total = total + inverses[block, 4 * i + j] * entries[j][:, cells]
                halves.append(total)
            last = jnp.concatenate(halves, axis=1)
            solved[4 * block + i] = last
        return last

    lax.fori_loop(0, BLOCKS, forward, jnp.zeros((16, NY), F32))

    def corrected(block, i, running):
        column = inverses[block, 4 * i + 3]
        return solved[4 * block + i] - jnp.concatenate([column, column], axis=1) * running

    def write(group):
        return pltpu.make_async_copy(
            staged.at[group], out.at[:, :, pl.ds(pl.multiple_of(8 * group, 8), 8), :], sems.at[group]
        )

    def backward(step, upper):
        group = 5 - step
        first = 2 * group
        running = upper
        pressure = [None] * 8
        for half in (1, 0):
            for i in range(4):
                pressure[4 * half + i] = corrected(first + half, i, running)
            running = pressure[4 * half]
        before = corrected(jnp.maximum(first - 1, 0), 3, running)
        before = jnp.where(group > 0, before, 0.0)
        pressure = [before] + pressure + [upper]
        for component in range(3):
            rows = []
            for z in range(8):
                here = pressure[z + 1]
                if component == 0:
                    slope = signed_x(here, scale_x)
                elif component == 1:
                    slope = signed_y(here, scale_y)
                else:
                    slope = 0.5 * (pressure[z + 2] - pressure[z])
                rows.append(spectrum[component, 8 * group + z] - slope)
            for r in range(16):
                sine, slot, inner = (r // 4) % 2, (r // 2) % 2, r % 2
                if r < 8:
                    mode = 4 * (2 * inner + (slot ^ parity[0])) + sine
                else:
                    mode = 4 * (r % 4) + 2 + sine
                staged[group, component, mode] = jnp.concatenate(
                    [rows[z][r : r + 1] for z in range(8)], axis=0
                )
        write(group).start()
        return running

    lax.fori_loop(0, 6, backward, jnp.zeros((16, NY), F32))
    for group in range(6):
        write(group).wait()


def across(parity, received, thrust, row_basis, wave_x, wave_y, inverses):
    tables = across_tables()
    smem = pl.BlockSpec(memory_space=pltpu.SMEM)
    vmem = pl.BlockSpec(memory_space=pltpu.VMEM)
    hbm = pl.BlockSpec(memory_space=pltpu.HBM)
    return pl.pallas_call(
        across_kernel,
        out_shape=jax.ShapeDtypeStruct((3, 16, NZ, NY), F32),
        in_specs=[smem] + [vmem] * 4 + [hbm] * 3,
        out_specs=hbm,
        scratch_shapes=[
            pltpu.VMEM((DESTS // 4, GROUP, 128), F32),
            pltpu.VMEM((BLOCKS, 16, 16, 256), F32),
            pltpu.VMEM((2, NY, NY), BF16),
            pltpu.VMEM((3, NZ, 16, NY), F32),
            pltpu.VMEM((NZ, 16, NY), F32),
            pltpu.VMEM((384, NY), BF16),
            pltpu.VMEM((384, NY), BF16),
            pltpu.VMEM((16, NY), F32),
            pltpu.VMEM((3, 4, 4, 1, NY), F32),
            pltpu.VMEM((6, 3, 16, 8, NY), F32),
            pltpu.SemaphoreType.DMA((12,)),
        ],
        compiler_params=pltpu.CompilerParams(vmem_limit_bytes=VMEM_BYTES),
        name="across",
    )(parity, thrust, row_basis, wave_x, wave_y, received, inverses, jnp.asarray(tables))


def body(adjoint, saved_grad, saved_u, disk_owner, disk_weight, row_x, thrust, block_inverse):
    axes = ("span", "stream")
    span = lax.axis_index("span")
    first_column = (5 * span // 4).astype(jnp.int32).reshape(1)
    sent = along(adjoint, saved_grad, saved_u, disk_owner, disk_weight, row_x, first_column)
    received = lax.all_to_all(
        sent.reshape(DESTS, 1, ROWS_SENT * 128), axes, split_axis=0, concat_axis=0, tiled=True
    ).reshape(DESTS // 4, GROUP, 128)

    device = lax.axis_index(axes).astype(jnp.int32)
    parity = device % 2
    row = jnp.arange(16, dtype=jnp.int32)
    sine, slot, inner = (row // 4) % 2, (row // 2) % 2, row % 2
    local = jnp.where(row < 8, 4 * inner + 2 * (slot ^ parity), 2 * (row % 4) + 1)
    mode = 8 * device + local
    wave = 2.0 * math.pi * mode.astype(F32) / NX
    wave_x = jnp.where(sine == 0, wave, -wave).reshape(2, 8, 1)
    wave_y = (2.0 * math.pi * jnp.arange(NY // 2, dtype=F32) / NY).reshape(1, 256)
    angle = (mode[:, None] * row_x[None, :] % NX).astype(F32) * (2.0 * math.pi / NX)
    basis = jnp.where(sine[:, None] == 0, jnp.cos(angle), jnp.sin(angle)) / math.sqrt(NX)
    row_basis = jnp.pad(basis, ((0, 0), (0, 128 - ROWS)))
    thrust_t = jnp.pad(thrust.T, ((0, 16 - COLS), (0, 128 - ROWS)))
    folded = block_inverse.reshape(2, 2, 2, BLOCKS, 16, 256)
    even = folded[:, :, 0].transpose(2, 3, 1, 0, 4)
    even = jnp.where(parity == 0, even, even[:, :, ::-1]).reshape(BLOCKS, 16, 1, 4, 256)
    odd = folded[:, :, 1].transpose(2, 3, 0, 1, 4).reshape(BLOCKS, 16, 1, 4, 256)
    inverses = jnp.concatenate([even, even, odd, odd], axis=2).reshape(BLOCKS, 16, 16, 256)
    return across(
        parity.reshape(1), received, thrust_t, row_basis, wave_x, wave_y, inverses
    )


def solution(mesh):
    in_specs = (
        P(None, "stream", "span", None),
        P(None, "stream", "span", None),
        P("stream", "span", None),
        P("stream", "span"),
        P("stream", "span"),
        P(),
        P(),
        P(("span", "stream"), None, None, None, None),
    )
    out_specs = P(None, ("span", "stream"), None, None)
    return jax.shard_map(body, mesh=mesh, in_specs=in_specs, out_specs=out_specs, check_vma=False)
```

time: 113 us -> 102 us (0.903)
  waiting for transfers between devices: 58.7 us -> 48.3 us
  Pallas kernels: 34.3 us -> 29.1 us
  other arithmetic: 1.29 us -> 4.23 us
  local copies, waits for them, and re-layouts: 6.17 us -> 8.26 us
    all_to_all x1, waiting for transfers between devices: 58.7 us -> 48.3 us  [body(): lax.all_to_all(sent.reshape(DESTS, 1, ROWS_SENT * 128), axes, split_axis=...]
    pallas_call x2, Pallas kernels: 34.3 us -> 29.1 us  [the longest x1 16 us: along(): pl.pallas_call(along_kernel, out_shape=jax.ShapeDtypeStruct((DESTS // 4,...]
    reshape x2 -> x4, local copies, waits for them, and re-layouts: 3.29 us -> 6.21 us  [the longest x1 2.73 us: body(): jnp.concatenate([even, even, odd, odd], axis=2).reshape(BLOCKS, 16, 16, 256)]
    concatenate x0 -> x1, other arithmetic: none -> 2.81 us  [body(): jnp.concatenate([even, even, odd, odd], axis=2).reshape(BLOCKS, 16, 16, 256)]
  transfers between devices with their start and end apart: 1 -> 1, of which waited for: 1 -> 1; matrix products, arithmetic and copies ran while one was open for 7% -> 12% of each run, Pallas kernels for 0% -> 0%
where the time goes in v2:
time: 102 us
  waiting for transfers between devices  48.3 us (47%)
  Pallas kernels  29.1 us (29%)
  starting transfers between devices  11.9 us (12%)
  local copies, waits for them, and re-layouts  8.26 us (8%)
  other arithmetic  4.23 us (4%)
    all_to_all x1, waiting for transfers between devices, body(): lax.all_to_all(sent.reshape(DESTS, 1, ROWS_SENT * 128), axes, split_axis=...  48.3 us
    pallas_call x1, Pallas kernels, along(): pl.pallas_call(along_kernel, out_shape=jax.ShapeDtypeStruct((DESTS // 4,...  16 us
    pallas_call x1, Pallas kernels, across(): pl.pallas_call(across_kernel, out_shape=jax.ShapeDtypeStruct((3, 16, NZ,...  13.1 us
    all_to_all x1, starting transfers between devices, body(): lax.all_to_all(sent.reshape(DESTS, 1, ROWS_SENT * 128), axes, split_axis=...  11.9 us
    concatenate x1, other arithmetic, body(): jnp.concatenate([even, even, odd, odd], axis=2).reshape(BLOCKS, 16, 16, 256)  2.81 us
    reshape x1, local copies, waits for them, and re-layouts, body(): jnp.concatenate([even, even, odd, odd], axis=2).reshape(BLOCKS, 16, 16, 256)  2.73 us
  transfers between devices with their start and end apart: 1, of which 1 were waited for; matrix products, arithmetic and copies ran while one was open for 12% of the time, Pallas kernels for 0%

profile of v2, /device:TPU:1, one launch (start us, length us, event | category | flops | bytes accessed | tf_op | source)
XLA Modules:
  0.0 102.1 jit_solution(11056293439455501204)
XLA Ops:
  0.0 16.0 %along.1 = f32[32,296,128]{2,1,0:T(8,128)} custom-call(s32[10]{0:T(128)} %row_x.1, s32[1]{0:T(128)} %bitcast.2.first_column, s32[3,64]{1,0:T(4,128)} %owner.1, f32[3,64]{1,0:T(4,128)} %weight.1, bf16[3,3,64,2048]{3,2,1,0:T(8,128)(2,1)} %adjoint_hbm.1, bf16[9,3,64,2048]{3,2,1,0:T(8,128)(2,1)} %grad_hbm.1, bf16[3,64,2048]{2,1,0:T(8,128)(2,1)} %saved_u_hbm.1, ...), custom_call_target="tpu_custom_call" | custom-call | tf_op jit(solution)/shard_map/along/pallas_call | solution.py:243
  16.0 0.0 copy-start.1
  16.0 0.0 copy-start.2
  16.0 0.0 copy-start
  16.1 11.9 %all-to-all-start = ((f32[128,1,9472]{2,1,0:T(1,128)}), f32[128,1,9472]{2,1,0:T(1,128)}, u32[]{:S(2)}, u32[]{:S(2)}) async-start(f32[128,1,9472]{2,1,0:T(1,128)} %bitcast.14), calls=%async_computation | async-start | bytes 9699328 | tf_op jit(solution)/shard_map/all_to_all | solution.py:499
  28.0 0.0 copy-done.1
  28.0 0.1 copy.15
  28.1 0.6 pad.8.thrust
  28.7 0.0 copy-done.2
  28.7 0.1 select_multiply_fusion
  28.9 0.6 pad.9.row_basis
  29.5 0.0 copy-done
  29.5 0.5 reshape.359
  30.0 0.1 slice_bitcast_fusion
  30.1 1.4 %copy.19 = f32[12,16,1,4,256]{4,3,2,1,0:T(4,128)} copy(f32[12,16,1,4,256]{4,1,0,3,2:T(8,128)S(1)} %bitcast.15) | data formatting | bytes 1572864 | tf_op jit(solution)/shard_map/reshape | solution.py:519
  31.5 0.1 reverse_select_fusion
  31.6 0.6 copy.17
  32.2 1.5 %reshape.360 = f32[12,16,1,4,256]{4,3,2,1,0:T(4,128)} reshape(f32[12,16,2,2,256]{4,3,2,1,0:T(2,128)S(1)} %copy.17) | data formatting | bytes 1572864 | tf_op jit(solution)/shard_map/reshape | solution.py:518
  33.8 2.8 %pad_maximum_fusion = f32[12,16,4,4,256]{4,3,2,1,0:T(4,128)S(1)} fusion(f32[12,16,1,4,256]{4,3,2,1,0:T(4,128)} %copy.19, f32[12,16,1,4,256]{4,3,2,1,0:T(4,128)} %reshape.360), kind=kLoop, calls=%fused_computation | loop fusion | flops 2359296 | bytes 4718592 | tf_op jit(solution)/shard_map/concatenate | solution.py:520
  36.6 2.7 %reshape.362.inverses_hbm = f32[12,16,16,256]{3,2,1,0:T(8,128)} reshape(f32[12,16,4,4,256]{4,3,2,1,0:T(4,128)S(1)} %pad_maximum_fusion) | data formatting | bytes 6291456 | tf_op jit(solution)/shard_map/reshape | solution.py:520
  39.3 0.6 iota_multiply_fusion.wave_y
  39.9 0.6 negate_select_fusion.wave_x
  40.5 48.3 %all-to-all-done = f32[128,1,9472]{2,1,0:T(1,128)} async-done(((f32[128,1,9472]{2,1,0:T(1,128)}), f32[128,1,9472]{2,1,0:T(1,128)}, u32[]{:S(2)}, u32[]{:S(2)}) %all-to-all-start) | async-done | bytes 4849696 | tf_op jit(solution)/shard_map/all_to_all | solution.py:499
  88.8 13.1 %across.1 = f32[3,16,48,512]{3,2,1,0:T(8,128)} custom-call(s32[1]{0:T(128)} %bitcast.parity, f32[16,128]{1,0:T(8,128)} %pad.8.thrust, f32[16,128]{1,0:T(8,128)} %pad.9.row_basis, f32[2,8,1]{2,1,0:T(8,128)} %negate_select_fusion.wave_x, f32[1,256]{1,0:T(1,128)} %iota_multiply_fusion.wave_y, f32[32,296,128]{2,1,0:T(8,128)} %bitcast.4.received_hbm, ...), custom_call_target="tpu_custom_call" | custom-call | tf_op jit(solution)/shard_map/across/pallas_call | solution.py:471
  (2 shorter events, 0.0 us)
Async XLA Ops:
  16.0 12.0 %copy-start.1 = (f32[10,10]{1,0:T(8,128)S(1)}, f32[10,10]{1,0:T(8,128)}, u32[]{:S(2)}) copy-start(f32[10,10]{1,0:T(8,128)} %param.17) | copy-start | bytes 1204
  16.0 12.7 %copy-start.2 = (s32[10]{0:T(128)S(1)}, s32[10]{0:T(128)}, u32[]{:S(2)}) copy-start(s32[10]{0:T(128)} %row_x.1) | copy-start | bytes 124
  16.0 13.4 %copy-start = (f32[8,12,4,4,256]{4,3,2,1,0:T(4,128)S(1)}, f32[8,12,4,4,256]{4,3,2,1,0:T(4,128)}, u32[]{:S(2)}) copy-start(f32[8,12,4,4,256]{4,3,2,1,0:T(4,128)} %param.18) | copy-start | bytes 4718596
  16.1 72.8 %all-to-all-start = ((f32[128,1,9472]{2,1,0:T(1,128)}), f32[128,1,9472]{2,1,0:T(1,128)}, u32[]{:S(2)}, u32[]{:S(2)}) async-start(f32[128,1,9472]{2,1,0:T(1,128)} %bitcast.14), calls=%async_computation | async-start | bytes 9699328 | tf_op jit(solution)/shard_map/all_to_all | solution.py:499

commit v3 on v2

v3 whole, which is shorter than its diff:
```python
import functools
import math

import jax
import jax.numpy as jnp
import ml_dtypes
import numpy as np
from jax import lax
from jax.experimental import pallas as pl
from jax.experimental.pallas import tpu as pltpu
from jax.sharding import PartitionSpec as P

NX = 2048
NY = 512
NZ = 48
ROWS = 10
COLS = 10
HALF = NX // 2
BLOCKS = NZ // 4
DESTS = 128
ROWS_SENT = 74
GROUP = 4 * ROWS_SENT
F32 = jnp.float32
BF16 = jnp.bfloat16
VMEM_BYTES = 58 * 1024 * 1024


def split_table(values):
    high = values.astype(ml_dtypes.bfloat16)
    low = (values - high.astype(np.float64)).astype(ml_dtypes.bfloat16)
    return high, low


def wave_rows(mode, sine, length):
    phase = mode[:, None] * np.arange(length)[None, :] % NX
    angle = phase * (2.0 * np.pi / NX)
    return np.where(sine[:, None] == 0, np.cos(angle), np.sin(angle)) / np.sqrt(NX)


@functools.lru_cache(maxsize=None)
def along_tables():
    row = np.arange(HALF)
    sine, rest = (row // 4) % 2, row % 4
    odd = wave_rows(8 * (row // 8) + 2 * rest + 1, sine, HALF)
    row = np.arange(HALF // 2)
    sine, slot, inner = (row // 4) % 2, (row // 2) % 2, row % 2
    even = [
        wave_rows(8 * (2 * (row // 8) + (slot ^ kind)) + 4 * inner + 2 * kind, sine, HALF // 2)
        for kind in range(2)
    ]
    odd = np.stack(split_table(odd)).transpose(0, 2, 1).reshape(2, HALF, 2, HALF // 2)
    even = np.stack(split_table(np.stack(even))).transpose(1, 0, 3, 2)
    even = even.reshape(2, 2, HALF // 2, 2, HALF // 4)
    return odd.transpose(2, 0, 1, 3), even.transpose(3, 0, 1, 2, 4)


@functools.lru_cache(maxsize=None)
def across_tables():
    basis = np.arange(NY)
    phase = np.arange(NY)[:, None] * (basis % (NY // 2))[None, :] % NY
    angle = phase * (2.0 * np.pi / NY)
    values = np.where((basis // (NY // 2))[None, :] == 0, np.cos(angle), np.sin(angle))
    return np.stack(split_table(values / np.sqrt(NY)))


def split(value):
    high = value.astype(BF16)
    return high, (value - high.astype(F32)).astype(BF16)


def dot_nt(left, right):
    return lax.dot_general(left, right, (((1,), (1,)), ((), ())), preferred_element_type=F32)


def dot_nn(left, right):
    return jnp.dot(left, right, preferred_element_type=F32)


def couple(level, step, adjoint, grad, source_high, source_low):
    quarter = NX // 4
    rows = pl.ds(pl.multiple_of(16 * step, 16), 16)
    for start in range(0, quarter, 128):
        lanes = [pl.ds(quarter * n + start, 128) for n in range(4)]
        velocity = [[adjoint[j, level, rows, l].astype(F32) for l in lanes] for j in range(3)]
        for i in range(3):
            value = []
            for n, l in enumerate(lanes):
                total = velocity[0][n] * grad[3 * i, level, rows, l].astype(F32)
                for j in range(1, 3):
                    total = total + velocity[j][n] * grad[3 * i + j, level, rows, l].astype(F32)
                value.append(total)
            first, second = value[0] + value[2], value[1] + value[3]
            folded = (value[0] - value[2], value[1] - value[3], first + second, first - second)
            target = pl.ds(pl.multiple_of(64 * (3 * level + i) + 16 * step, 16), 16)
            for n in range(4):
                high, low = split(folded[n])
                source_high[target, lanes[n]] = high
                source_low[target, lanes[n]] = low


def along_kernel(
    row_x, first_column, owner, weight, adjoint_hbm, grad_hbm, saved_u_hbm, odd_hbm, even_hbm,
    out, adjoint, grad, saved_u, odd, even, source_high, source_low, onehot, extra, outbox, sems,
):
    copies = []
    for level in range(3):
        copies.append(pltpu.make_async_copy(adjoint_hbm.at[:, level], adjoint.at[:, level], sems.at[2 * level]))
        copies.append(pltpu.make_async_copy(grad_hbm.at[:, level], grad.at[:, level], sems.at[2 * level + 1]))
    fetch_u = pltpu.make_async_copy(saved_u_hbm, saved_u, sems.at[6])

    def fetch_tables(step):
        return (
            pltpu.make_async_copy(odd_hbm.at[step], odd.at[step], sems.at[7 + 2 * step]),
            pltpu.make_async_copy(even_hbm.at[step], even.at[step], sems.at[8 + 2 * step]),
        )

    early, late = fetch_tables(0), fetch_tables(1)
    for copy in copies[:4]:
        copy.start()

    lane = lax.broadcasted_iota(jnp.int32, (1, 128), 1) % 16
    wanted = jnp.full((1, 128), -1, jnp.int32)
    for r in range(ROWS):
        wanted = jnp.where(lane == r, row_x[r], wanted)

    def mark(step, _):
        rows = pl.ds(pl.multiple_of(256 * step, 256), 256)
        cell = lax.broadcasted_iota(jnp.int32, (256, 128), 0) + 256 * step
        onehot[rows, :] = jnp.where(cell == wanted, 1.0, 0.0).astype(BF16)
        return 0

    lax.fori_loop(0, NX // 256, mark, 0)

    def couple_rows(level):
        def rows_of(step, _):
            couple(level, step, adjoint, grad, source_high, source_low)
            return 0

        lax.fori_loop(0, 4, rows_of, 0)

    sums_u, sums_a, masked = [], [], []

    def disk_level(level):
        column_u = dot_nn(saved_u[level], onehot[...])
        column_a = dot_nn(adjoint[0, level], onehot[...]).astype(BF16)
        column_u = jnp.where(lane == ROWS, 1.0, column_u).astype(BF16)
        own = owner[level : level + 1, :]
        heavy = weight[level : level + 1, :]
        masked.append(jnp.where(own >= 0, heavy, 0.0))
        row = lax.broadcasted_iota(jnp.int32, (8, 64), 0)
        rest = jnp.where(own == first_column[0] + row % 2, heavy, 0.0)
        for _ in range(3):
            part = rest.astype(BF16)
            rest = rest - part.astype(F32)
            sums_u.append(dot_nn(part, column_u))
            sums_a.append(dot_nn(part, column_a))

    def disk_rows():
        sum_u = functools.reduce(jnp.add, sums_u)
        sum_a = functools.reduce(jnp.add, sums_a)
        place = lax.broadcasted_iota(jnp.int32, (1, 128), 1) // 16
        sums = jnp.where(place == 4, sum_u[0:1], sum_u[1:2])
        sums = jnp.where(place == 6, sum_a[0:1], jnp.where(place == 7, sum_a[1:2], sums))
        last = jnp.concatenate([masked[2], jnp.zeros((1, 64), F32)], axis=1)
        last = jnp.where(place < 4, last, sums)
        return jnp.concatenate([jnp.concatenate(masked[:2], axis=1), last], axis=0)

    first_slot = lax.broadcasted_iota(jnp.int32, (8, 128), 0) % 4 < 2
    low_half = lax.broadcasted_iota(jnp.int32, (8, 128), 1) < 64

    def product(rows, span, high, low):
        cells = pl.ds(span, high.shape[0])
        result = dot_nn(source_high[rows, cells], high)
        result = result + dot_nn(source_low[rows, cells], high)
        return result + dot_nn(source_high[rows, cells], low)

    def send(step):
        part = pl.ds(16 * step, 16)
        return pltpu.make_async_copy(outbox.at[part], out.at[part], sems.at[11 + step])

    def fill(step, start, count, tiles):
        rows = pl.ds(start, count)

        def turned(value, tile, block):
            lanes = slice(128 * block, 128 * block + 128)
            begin = 128 * tile - start
            if tile < 4:
                part = value[begin : begin + 128, lanes]
            else:
                part = jnp.concatenate([value[begin : begin + 64, lanes]] * 2, axis=0)
            return part.T

        def store(dest, tile, value):
            place = ROWS_SENT * (dest % 4) + 8 * tile
            outbox[16 * step + dest // 4, pl.ds(place, 8), :] = value

        kinds = [
            product(rows, HALF + HALF // 2 * k, even[step, k, 0], even[step, k, 1]) for k in range(2)
        ]
        rest = product(rows, 0, odd[step, 0], odd[step, 1])
        for tile in tiles:
            for block in range(2):
                pair = [turned(value, tile, block) for value in kinds]
                for side in range(2):
                    single = turned(rest, tile, 2 * block + side)
                    for index in range(16):
                        dest = 32 * block + 16 * side + index
                        part = slice(8 * (dest // 2 % 16), 8 * (dest // 2 % 16) + 8)
                        even_part = jnp.where(first_slot, pair[dest % 2][part], pair[1 - dest % 2][part])
                        odd_part = single[8 * index : 8 * index + 8]
                        if tile < 4:
                            store(dest, tile, even_part)
                            store(dest, 4 + tile, odd_part)
                        else:
                            store(dest, 8, jnp.where(low_half, even_part, odd_part))

    def wait_for(level):
        copies[2 * level].wait()
        copies[2 * level + 1].wait()

    wait_for(0)
    for copy in early:
        copy.start()
    couple_rows(0)
    wait_for(1)
    fetch_u.start()
    for copy in copies[4:]:
        copy.start()
    couple_rows(1)
    for copy in early:
        copy.wait()
    for copy in late:
        copy.start()
    fetch_u.wait()
    fill(0, 0, 384, range(3))
    disk_level(0)
    disk_level(1)
    wait_for(2)
    for copy in late:
        copy.wait()
    for step in range(4):
        couple(2, step, adjoint, grad, source_high, source_low)
    disk_level(2)
    extra[...] = disk_rows()
    fill(1, 0, 384, range(3))

    def finish(step, _):
        for dest in range(64):
            outbox[16 * step + dest // 4, pl.ds(ROWS_SENT * (dest % 4) + 72, 2), :] = extra[...]
        fill(step, 384, 192, range(3, 5))
        send(step).start()
        return 0

    lax.fori_loop(0, 2, finish, 0)
    send(0).wait()
    send(1).wait()


def along(adjoint, grad, saved_u, owner, weight, row_x, first_column):
    odd, even = along_tables()
    smem = pl.BlockSpec(memory_space=pltpu.SMEM)
    vmem = pl.BlockSpec(memory_space=pltpu.VMEM)
    hbm = pl.BlockSpec(memory_space=pltpu.HBM)
    return pl.pallas_call(
        along_kernel,
        out_shape=jax.ShapeDtypeStruct((DESTS // 4, GROUP, 128), F32),
        in_specs=[smem, smem, vmem, vmem, hbm, hbm, hbm, hbm, hbm],
        out_specs=hbm,
        scratch_shapes=[
            pltpu.VMEM((3, 3, 64, NX), BF16),
            pltpu.VMEM((9, 3, 64, NX), BF16),
            pltpu.VMEM((3, 64, NX), BF16),
            pltpu.VMEM(odd.shape, BF16),
            pltpu.VMEM(even.shape, BF16),
            pltpu.VMEM((576, NX), BF16),
            pltpu.VMEM((576, NX), BF16),
            pltpu.VMEM((NX, 128), BF16),
            pltpu.VMEM((2, 128), F32),
            pltpu.VMEM((DESTS // 4, GROUP, 128), F32),
            pltpu.SemaphoreType.DMA((13,)),
        ],
        compiler_params=pltpu.CompilerParams(vmem_limit_bytes=VMEM_BYTES),
        name="along",
    )(row_x, first_column, owner, weight, adjoint, grad, saved_u, jnp.asarray(odd), jnp.asarray(even))


def signed_x(value, scale):
    return jnp.concatenate(
        [scale[c] * pltpu.roll(value[8 * c : 8 * c + 8], 4, 0) for c in range(2)], axis=0
    )


def signed_y(value, scale):
    return jnp.concatenate([scale * value[:, 256:], -scale * value[:, :256]], axis=1)


def across_kernel(
    parity, thrust, row_basis, wave_x, wave_y, received_hbm, inverses_hbm, tables_hbm,
    out, received, extras, inverses, tables, spectrum, solved, high_0, high_1, low_0, low_1, forced, heavy, turned, staged, sems,
):
    fetch_extras = []
    for t in range(4):
        window = pl.ds((ROWS_SENT * t + 72) // 8 * 8, 8)
        fetch_extras.append(
            pltpu.make_async_copy(received_hbm.at[:, :, window], extras.at[t], sems.at[12 + t])
        )
    fetch = [
        pltpu.make_async_copy(received_hbm.at[:, group], received.at[:, group], sems.at[6 + group])
        for group in range(4)
    ]
    fetch_tables = pltpu.make_async_copy(tables_hbm, tables, sems.at[10])
    fetch_inverses = pltpu.make_async_copy(inverses_hbm, inverses, sems.at[11])
    for copy in fetch_extras + [fetch[0], fetch_tables]:
        copy.start()
    grids = ((high_0, low_0), (high_1, low_1))
    low_half = lax.broadcasted_iota(jnp.int32, (1, 128), 1) < 64
    low_half3 = low_half[None]

    def place(unit, parts):
        high_grid, low_grid = grids[unit % 2]
        for n, (component, group) in enumerate(parts):
            for t in range(4):
                for inner in range(3):
                    pair = 3 * inner + component
                    target = pl.ds(192 * n + 16 * (3 * t + inner), 16)
                    for j in range(4):
                        cells = pl.ds(128 * j, 128)
                        values = []
                        for kind in range(2):
                            tile, side = (4 * kind + pair // 2, pair % 2) if pair < 8 else (8, kind)
                            rows = pl.ds(ROWS_SENT * t + 8 * tile, 8)
                            left = received[2 * j, group, rows, :]
                            right = received[2 * j + 1, group, rows, :]
                            if side == 0:
                                value = jnp.where(low_half, left, pltpu.roll(right, 64, 1))
                            else:
                                value = jnp.where(low_half, pltpu.roll(left, 64, 1), right)
                            if component == 0:
                                disk = heavy[inner, t, group, :, cells]
                                value = value + disk * forced[pl.ds(8 * kind, 8), cells]
                            values.append(value)
                        high, low = split(jnp.concatenate(values, axis=0))
                        high_grid[target, cells] = high
                        low_grid[target, cells] = low

    def multiply(unit, parts):
        high_grid, low_grid = grids[unit % 2]
        result = dot_nn(high_grid[...], tables[0])
        result = result + dot_nn(low_grid[...], tables[0])
        result = result + dot_nn(high_grid[...], tables[1])
        for n, (component, group) in enumerate(parts):
            spectrum[component, pl.ds(12 * group, 12)] = result[192 * n : 192 * n + 192].reshape(12, 16, NY)

    for copy in fetch_extras:
        copy.wait()
    for copy in [fetch[1], fetch_inverses] + fetch[2:]:
        copy.start()
    total = jnp.zeros((8, 1, 128), F32)
    for t in range(4):
        start = (ROWS_SENT * t + 72) % 8
        upper = extras[t, :, :, pl.ds(start, 1), :].reshape(4, 2, 4, 1, 128)
        lower = extras[t, :, :, pl.ds(start + 1, 1), :]
        total = total + jnp.sum(lower, axis=1)
        lower = lower.reshape(4, 2, 4, 1, 128)
        for j in range(4):
            cells = pl.ds(128 * j, 128)
            left, right = upper[j, 0], upper[j, 1]
            heavy[0, t, :, :, cells] = jnp.where(low_half3, left, pltpu.roll(right, 64, 2))
            heavy[1, t, :, :, cells] = jnp.where(low_half3, pltpu.roll(left, 64, 2), right)
            left, right = lower[j, 0], lower[j, 1]
            heavy[2, t, :, :, cells] = jnp.where(low_half3, left, pltpu.roll(right, 64, 2))
    column = lax.broadcasted_iota(jnp.int32, (16, 128), 0)
    sum_u = jnp.zeros((16, 128), F32)
    sum_a = jnp.zeros((16, 128), F32)
    for s in range(8):
        for other in range(2):
            hit = column == 5 * s // 4 + other
            sum_u = sum_u + jnp.where(hit, pltpu.roll(total[s], 64 - 16 * other, 1), 0.0)
            sum_a = sum_a + jnp.where(hit, pltpu.roll(total[s], 32 - 16 * other, 1), 0.0)
    lane = lax.broadcasted_iota(jnp.int32, (16, 128), 1)
    valid = (lane < ROWS) & (column < COLS)
    area = jnp.where(valid, sum_u[:, ROWS : ROWS + 1], 1.0)
    speed = sum_u / area
    reverse = sum_a / area
    coeff = jnp.where(valid, -thrust[...] * speed * (1.5 * speed + reverse), 0.0)
    cell = lax.broadcasted_iota(jnp.int32, (16, NY), 1)
    band = lax.broadcasted_iota(jnp.int32, (16, NY), 0)
    spread = jnp.where(cell * COLS // NY == band, 1.0, 0.0).astype(F32)
    exact = lax.Precision.HIGHEST
    per_column = lax.dot_general(
        row_basis[...], coeff, (((1,), (1,)), ((), ())), precision=exact, preferred_element_type=F32
    )
    forced[...] = jnp.dot(per_column, spread, precision=exact, preferred_element_type=F32)

    scale_x = [wave_x[c] for c in range(2)]
    scale_y = wave_y[0:1, :]

    def forward(block, carry):
        entries = []
        for i in range(4):
            z = 4 * block + i
            up = spectrum[2, z + 1] if z + 1 < NZ else 0.0
            down = spectrum[2, z - 1] if z > 0 else 0.0
            entries.append(
                signed_x(spectrum[0, z], scale_x)
                + signed_y(spectrum[1, z], scale_y)
                + 0.5 * (up - down)
            )
        entries[0] = entries[0] - carry
        last = None
        for i in range(4):
            halves = []
            for q in range(2):
                cells = slice(256 * q, 256 * q + 256)
                total = inverses[block, 4 * i] * entries[0][:, cells]
                for j in range(1, 4):
                    total = total + inverses[block, 4 * i + j] * entries[j][:, cells]
                halves.append(total)
            last = jnp.concatenate(halves, axis=1)
            solved[4 * block + i] = last
        return last

    parts = [[(component, group) for component in range(3)] for group in range(4)]
    carry = jnp.zeros((16, NY), F32)
    fetch[0].wait()
    place(0, parts[0])
    fetch_tables.wait()
    for group in range(4):
        if group < 3:
            fetch[group + 1].wait()
        if group == 1:
            fetch_inverses.wait()
        multiply(group, parts[group])
        if group < 3:
            place(group + 1, parts[group + 1])
        if group > 0:
            for block in range(max(3 * group - 4, 0), 3 * group - 1):
                carry = forward(block, carry)
    for block in range(8, BLOCKS):
        carry = forward(block, carry)

    def corrected(block, i, running):
        column = inverses[block, 4 * i + 3]
        return solved[4 * block + i] - jnp.concatenate([column, column], axis=1) * running

    def write(group):
        return pltpu.make_async_copy(
            staged.at[group], out.at[:, :, pl.ds(pl.multiple_of(8 * group, 8), 8), :], sems.at[group]
        )

    def backward(step, upper):
        group = 5 - step
        first = 2 * group
        running = upper
        pressure = [None] * 8
        for half in (1, 0):
            for i in range(4):
                pressure[4 * half + i] = corrected(first + half, i, running)
            running = pressure[4 * half]
        before = corrected(jnp.maximum(first - 1, 0), 3, running)
        before = jnp.where(group > 0, before, 0.0)
        pressure = [before] + pressure + [upper]
        for component in range(3):
            for z in range(8):
                here = pressure[z + 1]
                if component == 0:
                    slope = signed_x(here, scale_x)
                elif component == 1:
                    slope = signed_y(here, scale_y)
                else:
                    slope = 0.5 * (pressure[z + 2] - pressure[z])
                value = spectrum[component, 8 * group + z] - slope
                for j in range(4):
                    turned[component, j, pl.ds(16 * z, 16), :] = value[:, 128 * j : 128 * j + 128]
            for r in range(16):
                sine, slot, inner = (r // 4) % 2, (r // 2) % 2, r % 2
                if r < 8:
                    mode = 4 * (2 * inner + (slot ^ parity[0])) + sine
                else:
                    mode = 4 * (r % 4) + 2 + sine
                for j in range(4):
                    cells = pl.ds(128 * j, 128)
                    staged[group, component, mode, :, cells] = turned[component, j, pl.ds(r, 8, stride=16), :]
        write(group).start()
        return running

    lax.fori_loop(0, 6, backward, jnp.zeros((16, NY), F32))
    for group in range(6):
        write(group).wait()


def across(parity, received, thrust, row_basis, wave_x, wave_y, inverses):
    tables = across_tables()
    smem = pl.BlockSpec(memory_space=pltpu.SMEM)
    vmem = pl.BlockSpec(memory_space=pltpu.VMEM)
    hbm = pl.BlockSpec(memory_space=pltpu.HBM)
    return pl.pallas_call(
        across_kernel,
        out_shape=jax.ShapeDtypeStruct((3, 16, NZ, NY), F32),
        in_specs=[smem] + [vmem] * 4 + [hbm] * 3,
        out_specs=hbm,
        scratch_shapes=[
            pltpu.VMEM((8, 4, GROUP, 128), F32),
            pltpu.VMEM((4, 8, 4, 8, 128), F32),
            pltpu.VMEM((BLOCKS, 16, 16, 256), F32),
            pltpu.VMEM((2, NY, NY), BF16),
            pltpu.VMEM((3, NZ, 16, NY), F32),
            pltpu.VMEM((NZ, 16, NY), F32),
            pltpu.VMEM((576, NY), BF16),
            pltpu.VMEM((576, NY), BF16),
            pltpu.VMEM((576, NY), BF16),
            pltpu.VMEM((576, NY), BF16),
            pltpu.VMEM((16, NY), F32),
            pltpu.VMEM((3, 4, 4, 1, NY), F32),
            pltpu.VMEM((3, 4, 128, 128), F32),
            pltpu.VMEM((6, 3, 16, 8, NY), F32),
            pltpu.SemaphoreType.DMA((16,)),
        ],
        compiler_params=pltpu.CompilerParams(vmem_limit_bytes=VMEM_BYTES),
        name="across",
    )(parity, thrust, row_basis, wave_x, wave_y, received, inverses, jnp.asarray(tables))


def body(adjoint, saved_grad, saved_u, disk_owner, disk_weight, row_x, thrust, block_inverse):
    axes = ("span", "stream")
    span = lax.axis_index("span")
    first_column = (5 * span // 4).astype(jnp.int32).reshape(1)
    sent = along(adjoint, saved_grad, saved_u, disk_owner, disk_weight, row_x, first_column)
    received = lax.all_to_all(
        sent.reshape(DESTS, 1, ROWS_SENT * 128), axes, split_axis=0, concat_axis=0, tiled=True
    ).reshape(8, 4, GROUP, 128)

    device = lax.axis_index(axes).astype(jnp.int32)
    parity = device % 2
    row = jnp.arange(16, dtype=jnp.int32)
    sine, slot, inner = (row // 4) % 2, (row // 2) % 2, row % 2
    local = jnp.where(row < 8, 4 * inner + 2 * (slot ^ parity), 2 * (row % 4) + 1)
    mode = 8 * device + local
    wave = 2.0 * math.pi * mode.astype(F32) / NX
    wave_x = jnp.where(sine == 0, wave, -wave).reshape(2, 8, 1)
    wave_y = (2.0 * math.pi * jnp.arange(NY // 2, dtype=F32) / NY).reshape(1, 256)
    angle = (mode[:, None] * row_x[None, :] % NX).astype(F32) * (2.0 * math.pi / NX)
    basis = jnp.where(sine[:, None] == 0, jnp.cos(angle), jnp.sin(angle)) / math.sqrt(NX)
    row_basis = jnp.pad(basis, ((0, 0), (0, 128 - ROWS)))
    thrust_t = jnp.pad(thrust.T, ((0, 16 - COLS), (0, 128 - ROWS)))
    folded = block_inverse.reshape(2, 2, 2, BLOCKS, 16, 256)
    even = folded[:, :, 0].transpose(2, 3, 1, 0, 4)
    even = jnp.where(parity == 0, even, even[:, :, ::-1]).reshape(BLOCKS, 16, 1, 4, 256)
    odd = folded[:, :, 1].transpose(2, 3, 0, 1, 4).reshape(BLOCKS, 16, 1, 4, 256)
    inverses = jnp.concatenate([even, even, odd, odd], axis=2).reshape(BLOCKS, 16, 16, 256)
    return across(
        parity.reshape(1), received, thrust_t, row_basis, wave_x, wave_y, inverses
    )


def solution(mesh):
    in_specs = (
        P(None, "stream", "span", None),
        P(None, "stream", "span", None),
        P("stream", "span", None),
        P("stream", "span"),
        P("stream", "span"),
        P(),
        P(),
        P(("span", "stream"), None, None, None, None),
    )
    out_specs = P(None, ("span", "stream"), None, None)
    return jax.shard_map(body, mesh=mesh, in_specs=in_specs, out_specs=out_specs, check_vma=False)
```

time: 102 us -> 99.4 us (0.975)
  Pallas kernels: 29.1 us -> 26.2 us
    pallas_call x1, Pallas kernels: 13.1 us -> 11.6 us  [across(): pl.pallas_call(across_kernel, out_shape=jax.ShapeDtypeStruct((3, 16, NZ,...]
    pallas_call x1, Pallas kernels: 16 us -> 14.6 us  [along(): pl.pallas_call(along_kernel, out_shape=jax.ShapeDtypeStruct((DESTS // 4,...]
where the time goes in v3:
time: 99.4 us; the launch traced here: 99.2 us
  waiting for transfers between devices  48.5 us (49%)
  Pallas kernels  26.2 us (26%)
  starting transfers between devices  11.9 us (12%)
  local copies, waits for them, and re-layouts  8.26 us (8%)
  other arithmetic  4.03 us (4%)
    all_to_all x1, waiting for transfers between devices, body(): lax.all_to_all(sent.reshape(DESTS, 1, ROWS_SENT * 128), axes, split_axis=...  48.5 us
    pallas_call x1, Pallas kernels, along(): pl.pallas_call(along_kernel, out_shape=jax.ShapeDtypeStruct((DESTS // 4,...  14.6 us
    all_to_all x1, starting transfers between devices, body(): lax.all_to_all(sent.reshape(DESTS, 1, ROWS_SENT * 128), axes, split_axis=...  11.9 us
    pallas_call x1, Pallas kernels, across(): pl.pallas_call(across_kernel, out_shape=jax.ShapeDtypeStruct((3, 16, NZ,...  11.6 us
    reshape x1, local copies, waits for them, and re-layouts, body(): jnp.concatenate([even, even, odd, odd], axis=2).reshape(BLOCKS, 16, 16, 256)  2.73 us
    concatenate x1, other arithmetic, body(): jnp.concatenate([even, even, odd, odd], axis=2).reshape(BLOCKS, 16, 16, 256)  2.61 us
  transfers between devices with their start and end apart: 1, of which 1 were waited for; matrix products, arithmetic and copies ran while one was open for 12% of the time, Pallas kernels for 0%

profile of v3, /device:TPU:1, one launch (start us, length us, event | category | flops | bytes accessed | tf_op | source)
XLA Modules:
  0.0 99.2 jit_solution(5360699967278163958)
XLA Ops:
  0.0 14.6 %along.1 = f32[32,296,128]{2,1,0:T(8,128)} custom-call(s32[10]{0:T(128)} %row_x.1, s32[1]{0:T(128)} %bitcast.2.first_column, s32[3,64]{1,0:T(4,128)} %owner.1, f32[3,64]{1,0:T(4,128)} %weight.1, bf16[3,3,64,2048]{3,2,1,0:T(8,128)(2,1)} %adjoint_hbm.1, bf16[9,3,64,2048]{3,2,1,0:T(8,128)(2,1)} %grad_hbm.1, bf16[3,64,2048]{2,1,0:T(8,128)(2,1)} %saved_u_hbm.1, ...), custom_call_target="tpu_custom_call" | custom-call | tf_op jit(solution)/shard_map/along/pallas_call | solution.py:264
  14.6 0.0 copy-start.1
  14.6 0.0 copy-start.2
  14.6 0.0 copy-start
  14.6 11.9 %all-to-all-start = ((f32[128,1,9472]{2,1,0:T(1,128)}), f32[128,1,9472]{2,1,0:T(1,128)}, u32[]{:S(2)}, u32[]{:S(2)}) async-start(f32[128,1,9472]{2,1,0:T(1,128)} %bitcast.14), calls=%async_computation | async-start | bytes 9699328 | tf_op jit(solution)/shard_map/all_to_all | solution.py:529
  26.6 0.0 copy-done.1
  26.6 0.1 copy.15
  26.7 0.6 pad.8.thrust
  27.3 0.0 copy-done.2
  27.3 0.1 select_multiply_fusion
  27.4 0.6 pad.9.row_basis
  28.0 0.0 copy-done
  28.0 0.5 reshape.359
  28.6 0.1 slice_bitcast_fusion
  28.7 1.4 %copy.19 = f32[12,16,1,4,256]{4,3,2,1,0:T(4,128)} copy(f32[12,16,1,4,256]{4,1,0,3,2:T(8,128)S(1)} %bitcast.15) | data formatting | bytes 1572864 | tf_op jit(solution)/shard_map/reshape | solution.py:549
  30.1 0.1 reverse_select_fusion
  30.2 0.6 copy.17
  30.8 1.5 %reshape.360 = f32[12,16,1,4,256]{4,3,2,1,0:T(4,128)} reshape(f32[12,16,2,2,256]{4,3,2,1,0:T(2,128)S(1)} %copy.17) | data formatting | bytes 1572864 | tf_op jit(solution)/shard_map/reshape | solution.py:548
  32.4 2.6 %pad_maximum_fusion = f32[12,16,4,4,256]{4,3,2,1,0:T(4,128)S(1)} fusion(f32[12,16,1,4,256]{4,3,2,1,0:T(4,128)} %copy.19, f32[12,16,1,4,256]{4,3,2,1,0:T(4,128)} %reshape.360), kind=kLoop, calls=%fused_computation | loop fusion | flops 2359296 | bytes 4718592 | tf_op jit(solution)/shard_map/concatenate | solution.py:550
  35.0 2.7 %reshape.362.inverses_hbm = f32[12,16,16,256]{3,2,1,0:T(8,128)} reshape(f32[12,16,4,4,256]{4,3,2,1,0:T(4,128)S(1)} %pad_maximum_fusion) | data formatting | bytes 6291456 | tf_op jit(solution)/shard_map/reshape | solution.py:550
  37.7 0.6 iota_multiply_fusion.wave_y
  38.3 0.6 negate_select_fusion.wave_x
  38.9 48.5 %all-to-all-done = f32[128,1,9472]{2,1,0:T(1,128)} async-done(((f32[128,1,9472]{2,1,0:T(1,128)}), f32[128,1,9472]{2,1,0:T(1,128)}, u32[]{:S(2)}, u32[]{:S(2)}) %all-to-all-start) | async-done | bytes 4849696 | tf_op jit(solution)/shard_map/all_to_all | solution.py:529
  87.4 11.6 %across.1 = f32[3,16,48,512]{3,2,1,0:T(8,128)} custom-call(s32[1]{0:T(128)} %bitcast.parity, f32[16,128]{1,0:T(8,128)} %pad.8.thrust, f32[16,128]{1,0:T(8,128)} %pad.9.row_basis, f32[2,8,1]{2,1,0:T(8,128)} %negate_select_fusion.wave_x, f32[1,256]{1,0:T(1,128)} %iota_multiply_fusion.wave_y, f32[8,4,296,128]{3,2,1,0:T(8,128)} %bitcast.4.received_hbm, ...), custom_call_target="tpu_custom_call" | custom-call | tf_op jit(solution)/shard_map/across/pallas_call | solution.py:497
  (2 shorter events, 0.0 us)
Async XLA Ops:
  14.6 12.0 %copy-start.1 = (f32[10,10]{1,0:T(8,128)S(1)}, f32[10,10]{1,0:T(8,128)}, u32[]{:S(2)}) copy-start(f32[10,10]{1,0:T(8,128)} %param.17) | copy-start | bytes 1204
  14.6 12.7 %copy-start.2 = (s32[10]{0:T(128)S(1)}, s32[10]{0:T(128)}, u32[]{:S(2)}) copy-start(s32[10]{0:T(128)} %row_x.1) | copy-start | bytes 124
  14.6 13.4 %copy-start = (f32[8,12,4,4,256]{4,3,2,1,0:T(4,128)S(1)}, f32[8,12,4,4,256]{4,3,2,1,0:T(4,128)}, u32[]{:S(2)}) copy-start(f32[8,12,4,4,256]{4,3,2,1,0:T(4,128)} %param.18) | copy-start | bytes 4718596
  14.6 72.8 %all-to-all-start = ((f32[128,1,9472]{2,1,0:T(1,128)}), f32[128,1,9472]{2,1,0:T(1,128)}, u32[]{:S(2)}, u32[]{:S(2)}) async-start(f32[128,1,9472]{2,1,0:T(1,128)} %bitcast.14), calls=%async_computation | async-start | bytes 9699328 | tf_op jit(solution)/shard_map/all_to_all | solution.py:529

commit v4 on v3

--- a/solution.py
+++ b/solution.py
@@ -100,7 +100,7 @@
 
 def along_kernel(
     row_x, first_column, owner, weight, adjoint_hbm, grad_hbm, saved_u_hbm, odd_hbm, even_hbm,
-    out, adjoint, grad, saved_u, odd, even, source_high, source_low, onehot, extra, outbox, sems,
+    out, adjoint, grad, saved_u, odd, even, source_high, source_low, onehot, outbox, sems,
 ):
     copies = []
     for level in range(3):
@@ -115,7 +115,7 @@
         )
 
     early, late = fetch_tables(0), fetch_tables(1)
-    for copy in copies[:4]:
+    for copy in copies + [fetch_u] + list(early) + list(late):
         copy.start()
 
     lane = lax.broadcasted_iota(jnp.int32, (1, 128), 1) % 16
@@ -174,11 +174,11 @@
         result = result + dot_nn(source_low[rows, cells], high)
         return result + dot_nn(source_high[rows, cells], low)
 
-    def send(step):
-        part = pl.ds(16 * step, 16)
-        return pltpu.make_async_copy(outbox.at[part], out.at[part], sems.at[11 + step])
-
-    def fill(step, start, count, tiles):
+    def send(step, block):
+        part = pl.ds(16 * step + 8 * block, 8)
+        return pltpu.make_async_copy(outbox.at[part], out.at[part], sems.at[11 + 2 * step + block])
+
+    def fill(step, start, count, tiles, extra=None):
         rows = pl.ds(start, count)
 
         def turned(value, tile, block):
@@ -197,12 +197,13 @@
         kinds = [
             product(rows, HALF + HALF // 2 * k, even[step, k, 0], even[step, k, 1]) for k in range(2)
         ]
-        rest = product(rows, 0, odd[step, 0], odd[step, 1])
-        for tile in tiles:
-            for block in range(2):
+        for block in range(2):
+            modes = pl.ds(256 * block, 256)
+            rest = product(rows, 0, odd[step, 0, :, modes], odd[step, 1, :, modes])
+            for tile in tiles:
                 pair = [turned(value, tile, block) for value in kinds]
                 for side in range(2):
-                    single = turned(rest, tile, 2 * block + side)
+                    single = turned(rest, tile, side)
                     for index in range(16):
                         dest = 32 * block + 16 * side + index
                         part = slice(8 * (dest // 2 % 16), 8 * (dest // 2 % 16) + 8)
@@ -213,47 +214,37 @@
                             store(dest, 4 + tile, odd_part)
                         else:
                             store(dest, 8, jnp.where(low_half, even_part, odd_part))
+            if extra is not None:
+                for dest in range(32 * block, 32 * block + 32):
+                    outbox[16 * step + dest // 4, pl.ds(ROWS_SENT * (dest % 4) + 72, 2), :] = extra
+                send(step, block).start()
 
     def wait_for(level):
         copies[2 * level].wait()
         copies[2 * level + 1].wait()
 
     wait_for(0)
-    for copy in early:
-        copy.start()
     couple_rows(0)
     wait_for(1)
-    fetch_u.start()
-    for copy in copies[4:]:
-        copy.start()
     couple_rows(1)
-    for copy in early:
-        copy.wait()
-    for copy in late:
-        copy.start()
     fetch_u.wait()
-    fill(0, 0, 384, range(3))
     disk_level(0)
     disk_level(1)
     wait_for(2)
-    for copy in late:
+    for copy in early:
         copy.wait()
     for step in range(4):
         couple(2, step, adjoint, grad, source_high, source_low)
     disk_level(2)
-    extra[...] = disk_rows()
-    fill(1, 0, 384, range(3))
-
-    def finish(step, _):
-        for dest in range(64):
-            outbox[16 * step + dest // 4, pl.ds(ROWS_SENT * (dest % 4) + 72, 2), :] = extra[...]
-        fill(step, 384, 192, range(3, 5))
-        send(step).start()
-        return 0
-
-    lax.fori_loop(0, 2, finish, 0)
-    send(0).wait()
-    send(1).wait()
+    extra = disk_rows()
+    fill(0, 0, 384, range(3))
+    fill(0, 384, 192, range(3, 5), extra)
+    for copy in late:
+        copy.wait()
+    fill(1, 0, 576, range(5), extra)
+    for step in range(2):
+        for block in range(2):
+            send(step, block).wait()
 
 
 def along(adjoint, grad, saved_u, owner, weight, row_x, first_column):
@@ -275,9 +266,8 @@
             pltpu.VMEM((576, NX), BF16),
             pltpu.VMEM((576, NX), BF16),
             pltpu.VMEM((NX, 128), BF16),
-            pltpu.VMEM((2, 128), F32),
             pltpu.VMEM((DESTS // 4, GROUP, 128), F32),
-            pltpu.SemaphoreType.DMA((13,)),
+            pltpu.SemaphoreType.DMA((15,)),
         ],
         compiler_params=pltpu.CompilerParams(vmem_limit_bytes=VMEM_BYTES),
         name="along",
@@ -310,7 +300,7 @@
     ]
     fetch_tables = pltpu.make_async_copy(tables_hbm, tables, sems.at[10])
     fetch_inverses = pltpu.make_async_copy(inverses_hbm, inverses, sems.at[11])
-    for copy in fetch_extras + [fetch[0], fetch_tables]:
+    for copy in fetch_extras + [fetch[0], fetch_tables, fetch[1], fetch_inverses] + fetch[2:]:
         copy.start()
     grids = ((high_0, low_0), (high_1, low_1))
     low_half = lax.broadcasted_iota(jnp.int32, (1, 128), 1) < 64
@@ -353,8 +343,6 @@
 
     for copy in fetch_extras:
         copy.wait()
-    for copy in [fetch[1], fetch_inverses] + fetch[2:]:
-        copy.start()
     total = jnp.zeros((8, 1, 128), F32)
     for t in range(4):
         start = (ROWS_SENT * t + 72) % 8

time: 99.4 us -> 98.6 us (level)
  no operation moved by 1% of the time
where the time goes in v4:
time: 98.6 us; the launch traced here: 98.4 us
  waiting for transfers between devices  48.5 us (49%)
  Pallas kernels  25.4 us (26%)
  starting transfers between devices  11.9 us (12%)
  local copies, waits for them, and re-layouts  8.26 us (8%)
  other arithmetic  4.03 us (4%)
    all_to_all x1, waiting for transfers between devices, body(): lax.all_to_all(sent.reshape(DESTS, 1, ROWS_SENT * 128), axes, split_axis=...  48.5 us
    pallas_call x1, Pallas kernels, along(): pl.pallas_call(along_kernel, out_shape=jax.ShapeDtypeStruct((DESTS // 4,...  14.2 us
    all_to_all x1, starting transfers between devices, body(): lax.all_to_all(sent.reshape(DESTS, 1, ROWS_SENT * 128), axes, split_axis=...  11.9 us
    pallas_call x1, Pallas kernels, across(): pl.pallas_call(across_kernel, out_shape=jax.ShapeDtypeStruct((3, 16, NZ,...  11.2 us
    reshape x1, local copies, waits for them, and re-layouts, body(): jnp.concatenate([even, even, odd, odd], axis=2).reshape(BLOCKS, 16, 16, 256)  2.73 us
    concatenate x1, other arithmetic, body(): jnp.concatenate([even, even, odd, odd], axis=2).reshape(BLOCKS, 16, 16, 256)  2.61 us
  transfers between devices with their start and end apart: 1, of which 1 were waited for; matrix products, arithmetic and copies ran while one was open for 12% of the time, Pallas kernels for 0%

profile of v4, /device:TPU:1, one launch (start us, length us, event | category | flops | bytes accessed | tf_op | source)
XLA Modules:
  0.0 98.4 jit_solution(4943515379268967849)
XLA Ops:
  0.0 14.2 %along.1 = f32[32,296,128]{2,1,0:T(8,128)} custom-call(s32[10]{0:T(128)} %row_x.1, s32[1]{0:T(128)} %bitcast.2.first_column, s32[3,64]{1,0:T(4,128)} %owner.1, f32[3,64]{1,0:T(4,128)} %weight.1, bf16[3,3,64,2048]{3,2,1,0:T(8,128)(2,1)} %adjoint_hbm.1, bf16[9,3,64,2048]{3,2,1,0:T(8,128)(2,1)} %grad_hbm.1, bf16[3,64,2048]{2,1,0:T(8,128)(2,1)} %saved_u_hbm.1, ...), custom_call_target="tpu_custom_call" | custom-call | tf_op jit(solution)/shard_map/along/pallas_call | solution.py:255
  14.2 0.0 copy-start.1
  14.2 0.0 copy-start.2
  14.2 0.0 copy-start
  14.2 11.9 %all-to-all-start = ((f32[128,1,9472]{2,1,0:T(1,128)}), f32[128,1,9472]{2,1,0:T(1,128)}, u32[]{:S(2)}, u32[]{:S(2)}) async-start(f32[128,1,9472]{2,1,0:T(1,128)} %bitcast.14), calls=%async_computation | async-start | bytes 9699328 | tf_op jit(solution)/shard_map/all_to_all | solution.py:517
  26.1 0.0 copy-done.1
  26.2 0.1 copy.15
  26.3 0.6 pad.8.thrust
  26.9 0.0 copy-done.2
  26.9 0.1 select_multiply_fusion
  27.0 0.6 pad.9.row_basis
  27.6 0.0 copy-done
  27.6 0.5 reshape.359
  28.2 0.1 slice_bitcast_fusion
  28.3 1.4 %copy.19 = f32[12,16,1,4,256]{4,3,2,1,0:T(4,128)} copy(f32[12,16,1,4,256]{4,1,0,3,2:T(8,128)S(1)} %bitcast.15) | data formatting | bytes 1572864 | tf_op jit(solution)/shard_map/reshape | solution.py:537
  29.7 0.1 reverse_select_fusion
  29.8 0.6 copy.17
  30.4 1.5 %reshape.360 = f32[12,16,1,4,256]{4,3,2,1,0:T(4,128)} reshape(f32[12,16,2,2,256]{4,3,2,1,0:T(2,128)S(1)} %copy.17) | data formatting | bytes 1572864 | tf_op jit(solution)/shard_map/reshape | solution.py:536
  31.9 2.6 %pad_maximum_fusion = f32[12,16,4,4,256]{4,3,2,1,0:T(4,128)S(1)} fusion(f32[12,16,1,4,256]{4,3,2,1,0:T(4,128)} %copy.19, f32[12,16,1,4,256]{4,3,2,1,0:T(4,128)} %reshape.360), kind=kLoop, calls=%fused_computation | loop fusion | flops 2359296 | bytes 4718592 | tf_op jit(solution)/shard_map/concatenate | solution.py:538
  34.6 2.7 %reshape.362.inverses_hbm = f32[12,16,16,256]{3,2,1,0:T(8,128)} reshape(f32[12,16,4,4,256]{4,3,2,1,0:T(4,128)S(1)} %pad_maximum_fusion) | data formatting | bytes 6291456 | tf_op jit(solution)/shard_map/reshape | solution.py:538
  37.3 0.6 iota_multiply_fusion.wave_y
  37.9 0.6 negate_select_fusion.wave_x
  38.5 48.5 %all-to-all-done = f32[128,1,9472]{2,1,0:T(1,128)} async-done(((f32[128,1,9472]{2,1,0:T(1,128)}), f32[128,1,9472]{2,1,0:T(1,128)}, u32[]{:S(2)}, u32[]{:S(2)}) %all-to-all-start) | async-done | bytes 4849696 | tf_op jit(solution)/shard_map/all_to_all | solution.py:517
  87.0 11.2 %across.1 = f32[3,16,48,512]{3,2,1,0:T(8,128)} custom-call(s32[1]{0:T(128)} %bitcast.parity, f32[16,128]{1,0:T(8,128)} %pad.8.thrust, f32[16,128]{1,0:T(8,128)} %pad.9.row_basis, f32[2,8,1]{2,1,0:T(8,128)} %negate_select_fusion.wave_x, f32[1,256]{1,0:T(1,128)} %iota_multiply_fusion.wave_y, f32[8,4,296,128]{3,2,1,0:T(8,128)} %bitcast.4.received_hbm, ...), custom_call_target="tpu_custom_call" | custom-call | tf_op jit(solution)/shard_map/across/pallas_call | solution.py:485
  (2 shorter events, 0.0 us)
Async XLA Ops:
  14.2 12.0 %copy-start.1 = (f32[10,10]{1,0:T(8,128)S(1)}, f32[10,10]{1,0:T(8,128)}, u32[]{:S(2)}) copy-start(f32[10,10]{1,0:T(8,128)} %param.17) | copy-start | bytes 1204
  14.2 12.7 %copy-start.2 = (s32[10]{0:T(128)S(1)}, s32[10]{0:T(128)}, u32[]{:S(2)}) copy-start(s32[10]{0:T(128)} %row_x.1) | copy-start | bytes 124
  14.2 13.4 %copy-start = (f32[8,12,4,4,256]{4,3,2,1,0:T(4,128)S(1)}, f32[8,12,4,4,256]{4,3,2,1,0:T(4,128)}, u32[]{:S(2)}) copy-start(f32[8,12,4,4,256]{4,3,2,1,0:T(4,128)} %param.18) | copy-start | bytes 4718596
  14.2 72.8 %all-to-all-start = ((f32[128,1,9472]{2,1,0:T(1,128)}), f32[128,1,9472]{2,1,0:T(1,128)}, u32[]{:S(2)}, u32[]{:S(2)}) async-start(f32[128,1,9472]{2,1,0:T(1,128)} %bitcast.14), calls=%async_computation | async-start | bytes 9699328 | tf_op jit(solution)/shard_map/all_to_all | solution.py:517

commit v5 on v4

--- a/solution.py
+++ b/solution.py
@@ -431,9 +431,11 @@
         column = inverses[block, 4 * i + 3]
         return solved[4 * block + i] - jnp.concatenate([column, column], axis=1) * running
 
-    def write(group):
+    def write(group, component):
         return pltpu.make_async_copy(
-            staged.at[group], out.at[:, :, pl.ds(pl.multiple_of(8 * group, 8), 8), :], sems.at[group]
+            staged.at[group, component],
+            out.at[component, :, pl.ds(pl.multiple_of(8 * group, 8), 8), :],
+            sems.at[16 + 3 * group + component],
         )
 
     def backward(step, upper):
@@ -469,12 +471,13 @@
                 for j in range(4):
                     cells = pl.ds(128 * j, 128)
                     staged[group, component, mode, :, cells] = turned[component, j, pl.ds(r, 8, stride=16), :]
-        write(group).start()
+            write(group, component).start()
         return running
 
     lax.fori_loop(0, 6, backward, jnp.zeros((16, NY), F32))
     for group in range(6):
-        write(group).wait()
+        for component in range(3):
+            write(group, component).wait()
 
 
 def across(parity, received, thrust, row_basis, wave_x, wave_y, inverses):
@@ -502,7 +505,7 @@
             pltpu.VMEM((3, 4, 4, 1, NY), F32),
             pltpu.VMEM((3, 4, 128, 128), F32),
             pltpu.VMEM((6, 3, 16, 8, NY), F32),
-            pltpu.SemaphoreType.DMA((16,)),
+            pltpu.SemaphoreType.DMA((34,)),
         ],
         compiler_params=pltpu.CompilerParams(vmem_limit_bytes=VMEM_BYTES),
         name="across",

time: 98.6 us -> 98.6 us (level)
  no operation moved by 1% of the time
where the time goes in v5:
time: 98.6 us; the launch traced here: 98.4 us
  waiting for transfers between devices  48.5 us (49%)
  Pallas kernels  25.4 us (26%)
  starting transfers between devices  11.9 us (12%)
  local copies, waits for them, and re-layouts  8.26 us (8%)
  other arithmetic  4.03 us (4%)
    all_to_all x1, waiting for transfers between devices, body(): lax.all_to_all(sent.reshape(DESTS, 1, ROWS_SENT * 128), axes, split_axis=...  48.5 us
    pallas_call x1, Pallas kernels, along(): pl.pallas_call(along_kernel, out_shape=jax.ShapeDtypeStruct((DESTS // 4,...  14.2 us
    all_to_all x1, starting transfers between devices, body(): lax.all_to_all(sent.reshape(DESTS, 1, ROWS_SENT * 128), axes, split_axis=...  11.9 us
    pallas_call x1, Pallas kernels, across(): pl.pallas_call(across_kernel, out_shape=jax.ShapeDtypeStruct((3, 16, NZ,...  11.2 us
    reshape x1, local copies, waits for them, and re-layouts, body(): jnp.concatenate([even, even, odd, odd], axis=2).reshape(BLOCKS, 16, 16, 256)  2.73 us
    concatenate x1, other arithmetic, body(): jnp.concatenate([even, even, odd, odd], axis=2).reshape(BLOCKS, 16, 16, 256)  2.61 us
  transfers between devices with their start and end apart: 1, of which 1 were waited for; matrix products, arithmetic and copies ran while one was open for 12% of the time, Pallas kernels for 0%

profile of v5, /device:TPU:1, one launch (start us, length us, event | category | flops | bytes accessed | tf_op | source)
XLA Modules:
  0.0 98.4 jit_solution(5577082601187626340)
XLA Ops:
  0.0 14.2 %along.1 = f32[32,296,128]{2,1,0:T(8,128)} custom-call(s32[10]{0:T(128)} %row_x.1, s32[1]{0:T(128)} %bitcast.2.first_column, s32[3,64]{1,0:T(4,128)} %owner.1, f32[3,64]{1,0:T(4,128)} %weight.1, bf16[3,3,64,2048]{3,2,1,0:T(8,128)(2,1)} %adjoint_hbm.1, bf16[9,3,64,2048]{3,2,1,0:T(8,128)(2,1)} %grad_hbm.1, bf16[3,64,2048]{2,1,0:T(8,128)(2,1)} %saved_u_hbm.1, ...), custom_call_target="tpu_custom_call" | custom-call | tf_op jit(solution)/shard_map/along/pallas_call | solution.py:255
  14.2 0.0 copy-start.1
  14.2 0.0 copy-start.2
  14.2 0.0 copy-start
  14.2 11.9 %all-to-all-start = ((f32[128,1,9472]{2,1,0:T(1,128)}), f32[128,1,9472]{2,1,0:T(1,128)}, u32[]{:S(2)}, u32[]{:S(2)}) async-start(f32[128,1,9472]{2,1,0:T(1,128)} %bitcast.14), calls=%async_computation | async-start | bytes 9699328 | tf_op jit(solution)/shard_map/all_to_all | solution.py:520
  26.1 0.0 copy-done.1
  26.2 0.1 copy.15
  26.3 0.6 pad.8.thrust
  26.9 0.0 copy-done.2
  26.9 0.1 select_multiply_fusion
  27.0 0.6 pad.9.row_basis
  27.6 0.0 copy-done
  27.6 0.5 reshape.359
  28.2 0.1 slice_bitcast_fusion
  28.3 1.4 %copy.19 = f32[12,16,1,4,256]{4,3,2,1,0:T(4,128)} copy(f32[12,16,1,4,256]{4,1,0,3,2:T(8,128)S(1)} %bitcast.15) | data formatting | bytes 1572864 | tf_op jit(solution)/shard_map/reshape | solution.py:540
  29.7 0.1 reverse_select_fusion
  29.8 0.6 copy.17
  30.4 1.5 %reshape.360 = f32[12,16,1,4,256]{4,3,2,1,0:T(4,128)} reshape(f32[12,16,2,2,256]{4,3,2,1,0:T(2,128)S(1)} %copy.17) | data formatting | bytes 1572864 | tf_op jit(solution)/shard_map/reshape | solution.py:539
  31.9 2.6 %pad_maximum_fusion = f32[12,16,4,4,256]{4,3,2,1,0:T(4,128)S(1)} fusion(f32[12,16,1,4,256]{4,3,2,1,0:T(4,128)} %copy.19, f32[12,16,1,4,256]{4,3,2,1,0:T(4,128)} %reshape.360), kind=kLoop, calls=%fused_computation | loop fusion | flops 2359296 | bytes 4718592 | tf_op jit(solution)/shard_map/concatenate | solution.py:541
  34.6 2.7 %reshape.362.inverses_hbm = f32[12,16,16,256]{3,2,1,0:T(8,128)} reshape(f32[12,16,4,4,256]{4,3,2,1,0:T(4,128)S(1)} %pad_maximum_fusion) | data formatting | bytes 6291456 | tf_op jit(solution)/shard_map/reshape | solution.py:541
  37.3 0.6 iota_multiply_fusion.wave_y
  37.9 0.6 negate_select_fusion.wave_x
  38.5 48.5 %all-to-all-done = f32[128,1,9472]{2,1,0:T(1,128)} async-done(((f32[128,1,9472]{2,1,0:T(1,128)}), f32[128,1,9472]{2,1,0:T(1,128)}, u32[]{:S(2)}, u32[]{:S(2)}) %all-to-all-start) | async-done | bytes 4849696 | tf_op jit(solution)/shard_map/all_to_all | solution.py:520
  87.0 11.2 %across.1 = f32[3,16,48,512]{3,2,1,0:T(8,128)} custom-call(s32[1]{0:T(128)} %bitcast.parity, f32[16,128]{1,0:T(8,128)} %pad.8.thrust, f32[16,128]{1,0:T(8,128)} %pad.9.row_basis, f32[2,8,1]{2,1,0:T(8,128)} %negate_select_fusion.wave_x, f32[1,256]{1,0:T(1,128)} %iota_multiply_fusion.wave_y, f32[8,4,296,128]{3,2,1,0:T(8,128)} %bitcast.4.received_hbm, ...), custom_call_target="tpu_custom_call" | custom-call | tf_op jit(solution)/shard_map/across/pallas_call | solution.py:488
  (2 shorter events, 0.0 us)
Async XLA Ops:
  14.2 12.0 %copy-start.1 = (f32[10,10]{1,0:T(8,128)S(1)}, f32[10,10]{1,0:T(8,128)}, u32[]{:S(2)}) copy-start(f32[10,10]{1,0:T(8,128)} %param.17) | copy-start | bytes 1204
  14.2 12.7 %copy-start.2 = (s32[10]{0:T(128)S(1)}, s32[10]{0:T(128)}, u32[]{:S(2)}) copy-start(s32[10]{0:T(128)} %row_x.1) | copy-start | bytes 124
  14.2 13.4 %copy-start = (f32[8,12,4,4,256]{4,3,2,1,0:T(4,128)S(1)}, f32[8,12,4,4,256]{4,3,2,1,0:T(4,128)}, u32[]{:S(2)}) copy-start(f32[8,12,4,4,256]{4,3,2,1,0:T(4,128)} %param.18) | copy-start | bytes 4718596
  14.2 72.8 %all-to-all-start = ((f32[128,1,9472]{2,1,0:T(1,128)}), f32[128,1,9472]{2,1,0:T(1,128)}, u32[]{:S(2)}, u32[]{:S(2)}) async-start(f32[128,1,9472]{2,1,0:T(1,128)} %bitcast.14), calls=%async_computation | async-start | bytes 9699328 | tf_op jit(solution)/shard_map/all_to_all | solution.py:520
